TPU v7x, 128 devices: a whole 4x4x4 slice. The times are simulated.
128 devices in a mesh: grid: 16 (over x, z), mode: 8 (over y, core).
Axes of the slice: x: 4, y: 4, z: 4, core: 2. Of those that a mesh axis runs over, the one named last changes fastest.
Arguments:
- state: bfloat16 [2, 1024, 64, 4096], P(None, 'mode', 'grid'), may hold values from 0.049804688 to 2
- film_mask: int32 [64, 4096], P('grid'), may hold values 0 or 1
- basis: bfloat16 [2, 256, 64, 4096], P(None, 'mode', 'grid'), may hold values from -0.0078125 to 0.0078125
- sample_cells: int32 [16, 512], P('grid'), may hold values from 0 to 16383
- owner: int32 [16, 512, 1], P('grid'), may hold values from 0 to 127; in each aligned block of 512 rows (0 to 511, 512 to 1023, ..., all dimensions but the last counted through in order) at most 8 rows name the same one
Outputs:
- reduced_proj: float32 [256, 1024], P('grid', 'mode')
- sampled: bfloat16 [128, 128, 2560], P(('grid', 'mode'))
- hyper_gram: float32 [256, 256], P(('grid', 'mode'))
- hyper_proj: float32 [256, 1024], P(('grid', 'mode'))
Inputs may be any that keep to these rules, and one draw needn't show every extreme that they name: Among the 512 samples of one grid block, at most 8 share an owner.
All inputs are finite; a program needn't handle non-finite values. No bound on the sum of `film_mask` on one device may be relied on, other than what follows from the above.
Results may differ from a plain program's by a relative error of at most 0.0029.
Values may be sent and summed in bfloat16 or wider, within the bound.
A program may use at most 128 MiB of HBM per device.

v0:
```python
import jax
import jax.numpy as jnp
from jax import lax
from jax.sharding import PartitionSpec as P


def with_halo(block, sides, width):
    for axis, dim in sides:
        count = lax.axis_size(axis)
        forward = [(i, i + 1) for i in range(count - 1)]
        backward = [(target, source) for source, target in forward]
        low = lax.ppermute(
            lax.slice_in_dim(block, block.shape[dim] - width, None, axis=dim), axis, forward
        )
        high = lax.ppermute(lax.slice_in_dim(block, 0, width, axis=dim), axis, backward)
        block = jnp.concatenate([low, block, high], axis=dim)
    return block


def per_device(state, film_mask, basis, sample_cells, owner):
    n_grid = lax.axis_size("grid")
    n_mode = lax.axis_size("mode")
    devices = n_grid * n_mode
    modes_dev = basis.shape[1]
    snaps_dev = state.shape[1]
    row_count = state.shape[2]
    col_count = state.shape[3]
    cell_count = row_count * col_count
    sample_count = sample_cells.shape[1]
    capacity = 2 * sample_count // devices
    padded = with_halo(state[0], (("grid", 1),), 1)
    padded = jnp.pad(padded.astype(jnp.float32), ((0, 0), (0, 0), (1, 1)))
    substrate = padded[:, 1:-1, 1:-1]
    biomass = state[1].astype(jnp.float32)
    biofilm = film_mask.astype(jnp.float32)
    laplace = (
        padded[:, 2:, 1:-1]
        + padded[:, :-2, 1:-1]
        + padded[:, 1:-1, 2:]
        + padded[:, 1:-1, :-2]
        - 4.0 * substrate
    )
    uptake = substrate / (0.5 + substrate)
    sub_rate = (1.0 - 0.2 * biofilm) * laplace - 2.0 * biomass * uptake
    bio_rate = biofilm * (biomass * uptake - 0.1 * biomass)
    rate = jnp.stack([sub_rate, bio_rate]).astype(jnp.bfloat16)
    partial_proj = jnp.einsum(
        "skrc,snrc->kn",
        lax.all_gather(basis, "mode", axis=1, tiled=True),
        rate,
        preferred_element_type=jnp.float32,
    )
    reduced_proj = lax.psum_scatter(partial_proj, "grid", scatter_dimension=0, tiled=True)
    picked_cells = sample_cells[0]
    owners = owner[0, :, 0]
    onehot = (owners[:, None] == jnp.arange(devices, dtype=jnp.int32)[None, :]).astype(jnp.int32)
    slot_rank = jnp.sum((jnp.cumsum(onehot, axis=0) - 1) * onehot, axis=1)
    picked_basis = jnp.take(basis.reshape(2, modes_dev, cell_count), picked_cells, axis=2)
    picked_rate = jnp.take(rate.reshape(2, snaps_dev, cell_count), picked_cells, axis=2)
    rows = jnp.concatenate(
        [
            picked_basis.transpose(2, 0, 1).reshape(sample_count, 2 * modes_dev),
            picked_rate.transpose(2, 0, 1).reshape(sample_count, 2 * snaps_dev),
        ],
        axis=1,
    )
    row_width = rows.shape[1]
    send_buffer = (
        jnp.zeros((devices * capacity, row_width), jnp.bfloat16)
        .at[owners * capacity + slot_rank]
        .set(rows)
    )
    received = lax.all_to_all(
        send_buffer, ("grid", "mode"), split_axis=0, concat_axis=0, tiled=True
    ).reshape(n_grid, n_mode, capacity, row_width)
    own_rows = n_grid * capacity
    basis_part = received[..., : 2 * modes_dev].reshape(n_grid, n_mode, capacity, 2, modes_dev)
    basis_part = basis_part.transpose(0, 2, 3, 1, 4).reshape(own_rows, 2, n_mode * modes_dev)
    rate_part = received[..., 2 * modes_dev :].reshape(n_grid, n_mode, capacity, 2, snaps_dev)
    rate_part = rate_part.transpose(0, 2, 3, 1, 4).reshape(own_rows, 2, n_mode * snaps_dev)
    sampled = jnp.concatenate(
        [basis_part.reshape(own_rows, -1), rate_part.reshape(own_rows, -1)], axis=1
    )[None]
    weight_rows = cell_count / sample_count
    gram_part = weight_rows * jnp.einsum(
        "rsk,rsl->kl", basis_part, basis_part, preferred_element_type=jnp.float32
    )
    proj_part = weight_rows * jnp.einsum(
        "rsk,rsn->kn", basis_part, rate_part, preferred_element_type=jnp.float32
    )
    hyper_gram, hyper_proj = (
        lax.psum_scatter(gram_part, ("grid", "mode"), scatter_dimension=0, tiled=True),
        lax.psum_scatter(proj_part, ("grid", "mode"), scatter_dimension=0, tiled=True),
    )
    return (reduced_proj, sampled, hyper_gram, hyper_proj)


def solution(mesh):
    in_specs = (
        P(None, "mode", "grid", None),
        P("grid", None),
        P(None, "mode", "grid", None),
        P("grid", None),
        P("grid", None, None),
    )
    out_specs = (
        P("grid", "mode"),
        P(("grid", "mode"), None, None),
        P(("grid", "mode"), None),
        P(("grid", "mode"), None),
    )
    return jax.shard_map(
        per_device, mesh=mesh, in_specs=in_specs, out_specs=out_specs, check_vma=False
    )
```

profile of v0, /device:TPU:1, one launch (start us, length us, event | category | flops | bytes accessed | tf_op | source)
XLA Modules:
  0.0 400.7 jit_solution(4036985257953578801)
XLA Ops:
  8.0 0.0 all-gather.2.cloned.1.call-start
  8.0 4.0 %copy.59 = bf16[2,32,4,4096]{3,1,0,2:T(8,128)(2,1)} copy(bf16[2,32,4,4096]{3,2,1,0:T(4,128)(2,1)} %param.7) | data formatting | bytes 4194304 | tf_op args[2]
  12.1 0.0 all-gather.2.cloned.1.call-update
  12.1 8.1 %fusion.31 = (bf16[1,128,4,4096]{3,2,1,0:T(4,128)(2,1)S(1)}, bf16[1,128,4,4096]{3,2,1,0:T(4,128)(2,1)}) fusion(bf16[2,128,4,4096]{3,2,1,0:T(4,128)(2,1)} %param.5), kind=kLoop, calls=%fused_computation.65 | loop fusion | bytes 16777216 | tf_op jit(solution)/shard_map/slice | solution.py:31
  20.2 2.3 copy.95
  22.5 0.0 copy-start.1
  22.5 0.0 copy-start.3
  22.5 0.0 copy-start.5
  22.5 0.0 copy-start.4
  22.5 1.9 copy-done.1
  24.4 1.5 fusion.32
  25.9 4.5 %collective-permute-start = (bf16[128,1,4096]{2,0,1:T(8,128)(2,1)}, bf16[128,1,4096]{2,0,1:T(8,128)(2,1)S(1)}, u32[]{:S(2)}, u32[]{:S(2)}) collective-permute-start(bf16[128,1,4096]{2,0,1:T(8,128)(2,1)} %get-tuple-element.26), channel_id=1, source_target_pairs={{0,8},{8,16},{16,24},{24,32},{32,40},{40,48},{48,56},{56,64},{64,7... | collective-permute-start | bytes 3145736 | tf_op jit(solution)/shard_map/ppermute | solution.py:12
  30.4 1.5 collective-permute-start.1
  31.9 14.9 %copy.62 = bf16[2,32,4,4096]{1,0,3,2:T(2,128)(2,1)} copy(bf16[2,32,4,4096]{3,2,1,0:T(4,128)(2,1)S(1)} %copy-done.2) | data formatting | bytes 4194304 | tf_op args[2]
  46.8 0.0 copy-done.5
  46.8 5.0 %gather_fusion = bf16[512,2,32]{2,1,0:T(2,128)(2,1)S(1)} fusion(bf16[2,32,16384]{1,0,2:T(2,128)(2,1)} %bitcast.93, s32[1024]{0:T(1024)S(1)} %pad_clamp_fusion), kind=kCustom, calls=%fused_computation | custom fusion | bytes 133120 | tf_op jit(solution)/shard_map/jit(_take)/gather | solution.py:58
  51.8 1.8 broadcast_select_fusion.1
  53.6 0.1 copy.63
  53.7 0.1 copy.68
  53.8 0.0 copy-done.4
  53.8 0.1 copy.60
  54.0 0.2 fusion.27
  54.2 0.1 add_add_fusion
  54.3 0.2 fusion.26
  54.6 0.0 collective-permute-done
  54.6 2.0 collective-permute-done.1
  56.6 3.7 maximum_convert_fusion
  60.3 11.6 %fusion.5 = (bf16[128,4,4096]{2,0,1:T(8,128)(2,1)}, bf16[128,4,4096]{2,0,1:T(8,128)(2,1)}) fusion(f32[128,6,4096]{2,0,1:T(8,128)S(1)} %maximum_convert_fusion, f32[4,4096]{1,0:T(4,128)S(1)} %multiply_subtract_fusion, bf16[1,128,4,4096]{3,2,1,0:T(4,128)(2,1)} %get-tuple-element.25, f32[4,4096]{1,0:T(4,128)S(1)} %convert_element_type.21), kind=kLoop, calls=%fused_computation.14 | loop fusion | flops 37748736 | bytes 50462720 | tf_op jit(solution)/shard_map/convert.8
  71.9 6.4 %copy.64 = bf16[128,4,4096]{0,2,1:T(8,128)(2,1)} copy(bf16[128,4,4096]{2,0,1:T(8,128)(2,1)} %get-tuple-element.22) | data formatting | bytes 8388608 | tf_op jit(solution)/shard_map/convert.8
  78.3 8.7 %copy.66 = bf16[1,128,16384]{1,0,2:T(2,128)(2,1)} copy(bf16[1,128,16384]{1,2,0:T(8,128)(2,1)} %bitcast.91) | data formatting | bytes 8388608 | tf_op jit(solution)/shard_map/stack | solution.py:46
  87.0 6.3 %copy.65 = bf16[128,4,4096]{0,2,1:T(8,128)(2,1)} copy(bf16[128,4,4096]{2,0,1:T(8,128)(2,1)} %get-tuple-element.23) | data formatting | bytes 8388608 | tf_op jit(solution)/shard_map/convert.7
  93.3 7.9 %copy.67 = bf16[1,128,16384]{1,0,2:T(2,128)(2,1)S(1)} copy(bf16[1,128,16384]{1,2,0:T(8,128)(2,1)} %bitcast.92) | data formatting | bytes 8388608 | tf_op jit(solution)/shard_map/stack | solution.py:46
  101.2 0.0 copy-done
  101.2 0.0 copy-start.6
  101.2 20.3 %pad_maximum_fusion = bf16[2,128,16384]{1,0,2:T(2,128)(2,1)} fusion(bf16[1,128,16384]{1,0,2:T(2,128)(2,1)S(1)} %copy.67, bf16[1,128,16384]{1,0,2:T(2,128)(2,1)S(1)} %copy-done), kind=kLoop, calls=%fused_computation.24 | loop fusion | flops 16777216 | bytes 16777216 | tf_op jit(solution)/shard_map/stack | solution.py:46
  121.5 4.7 %gather_fusion.1 = bf16[512,2,128]{2,1,0:T(2,128)(2,1)S(1)} fusion(bf16[2,128,16384]{1,0,2:T(2,128)(2,1)} %pad_maximum_fusion, s32[1024]{0:T(1024)S(1)} %pad_clamp_fusion), kind=kCustom, calls=%fused_computation.1 | custom fusion | bytes 526336 | tf_op jit(solution)/shard_map/jit(_take)/gather | solution.py:59
  126.3 1.8 broadcast_select_fusion
  128.1 3.5 scatter_custom_fusion
  131.5 12.2 %all-to-all-start = ((bf16[128,8,320]{2,1,0:T(8,128)(2,1)}), bf16[128,8,320]{2,1,0:T(8,128)(2,1)S(1)}, u32[]{:S(2)}, u32[]{:S(2)}) async-start(bf16[128,8,320]{2,1,0:T(8,128)(2,1)} %bitcast.24), calls=%async_computation | async-start | bytes 1572864 | tf_op jit(solution)/shard_map/all_to_all | solution.py:73
  143.8 0.0 all-reduce.10.cloned.1.call-start
  143.8 0.6 dynamic-slice
  145.1 15.1 %all-to-all-done = bf16[128,8,320]{2,1,0:T(8,128)(2,1)S(1)} async-done(((bf16[128,8,320]{2,1,0:T(8,128)(2,1)}), bf16[128,8,320]{2,1,0:T(8,128)(2,1)S(1)}, u32[]{:S(2)}, u32[]{:S(2)}) %all-to-all-start) | async-done | bytes 655392 | tf_op jit(solution)/shard_map/all_to_all | solution.py:73
  160.2 0.2 reshape.132
  160.4 0.1 copy.71
  160.6 0.2 copy.69
  160.8 0.4 reshape.134
  161.2 0.4 reshape_reshape.6
  161.6 0.2 slice_bitcast_fusion
  161.8 0.1 copy.70
  162.0 0.2 reshape_reshape.7
  162.2 0.9 fusion.15
  163.2 1.5 fusion.14
  164.7 0.9 maximum_bitcast_fusion
  165.6 0.0 all-reduce.10.cloned.1.call-update
  165.6 0.0 all-reduce.8.cloned.1.call-start
  165.6 0.0 all-gather.2.cloned.1.call-done
  165.7 12.0 %fusion.16 = f32[256,128]{0,1:T(8,128)} fusion(bf16[2,256,4,4096]{3,1,0,2:T(8,128)(2,1)} %all-gather.2.cloned.1.call-done, bf16[1,128,4,4096]{3,1,0,2:T(8,128)(2,1)} %bitcast.90, bf16[1,128,4,4096]{3,1,0,2:T(8,128)(2,1)} %bitcast.89), kind=kOutput, calls=%fused_computation.32 | convolution fusion | flops 2151677952 | bytes 25296896 | tf_op jit(solution)/shard_map/skrc,snrc->kn/dot_general | solution.py:47
  177.6 0.0 all-reduce.8.cloned.1.call-update
  177.6 132.1 %all-reduce.10.cloned.1.call-done = (f32[256,256]{1,0:T(8,128)}, f32[256,1024]{1,0:T(8,128)}) async-done(((f32[256,256]{1,0:T(8,128)}, f32[256,1024]{1,0:T(8,128)}), (f32[256,256]{1,0:T(8,128)}, f32[256,1024]{1,0:T(8,128)})) %all-reduce.10.cloned.1.call-update) | async-done | bytes 1310736
  309.7 1.3 constant_dynamic-slice_fusion.1
  311.0 1.4 constant_dynamic-slice_fusion
  312.3 79.4 %all-reduce.8.cloned.1.call-done = f32[256,128]{0,1:T(8,128)} async-done(((f32[256,128]{0,1:T(8,128)}), f32[256,128]{0,1:T(8,128)}) %all-reduce.8.cloned.1.call-update) | async-done | bytes 131088
  391.7 0.9 constant_dynamic-slice_fusion.2
  392.6 0.7 copy.75
  (17 shorter events, 0.2 us)
Async XLA Ops:
  8.0 157.7 %all-gather.2.cloned.1.call-start = ((), (), s32[]{:S(2)}) async-start(), calls=%async_computation.1 | async-start | bytes 18874368 | tf_op jit(solution)/shard_map/all_gather | solution.py:49
  20.2 11.7 %copy-start.2 = (bf16[2,32,4,4096]{3,2,1,0:T(4,128)(2,1)S(1)}, bf16[2,32,4,4096]{3,2,1,0:T(4,128)(2,1)}, u32[]{:S(2)}) copy-start(bf16[2,32,4,4096]{3,2,1,0:T(4,128)(2,1)} %param.7) | copy-start | bytes 6291460
  22.5 2.0 copy-start.1
  22.5 24.3 %copy-start.3 = (s32[4,4096]{1,0:T(4,128)S(1)}, s32[4,4096]{1,0:T(4,128)}, u32[]{:S(2)}) copy-start(s32[4,4096]{1,0:T(4,128)} %param.6) | copy-start | bytes 196612
  22.5 24.3 %copy-start.5 = (s32[1,512]{1,0:T(1,128)S(1)}, s32[1,512]{1,0:T(1,128)}, u32[]{:S(2)}) copy-start(s32[1,512]{1,0:T(1,128)} %param.8) | copy-start | bytes 6148
  22.5 31.3 %copy-start.4 = (s32[1,512,1]{1,2,0:T(1,128)S(1)}, s32[1,512,1]{1,2,0:T(1,128)}, u32[]{:S(2)}) copy-start(s32[1,512,1]{1,2,0:T(1,128)} %param.9) | copy-start | bytes 6148
  25.9 28.7 %collective-permute-start = (bf16[128,1,4096]{2,0,1:T(8,128)(2,1)}, bf16[128,1,4096]{2,0,1:T(8,128)(2,1)S(1)}, u32[]{:S(2)}, u32[]{:S(2)}) collective-permute-start(bf16[128,1,4096]{2,0,1:T(8,128)(2,1)} %get-tuple-element.26), channel_id=1, source_target_pairs={{0,8},{8,16},{16,24},{24,32},{32,40},{40,48},{48,56},{56,64},{64,7... | collective-permute-start | bytes 3145736 | tf_op jit(solution)/shard_map/ppermute | solution.py:12
  30.4 26.2 %collective-permute-start.1 = (bf16[128,1,4096]{2,0,1:T(8,128)(2,1)}, bf16[128,1,4096]{2,0,1:T(8,128)(2,1)}, u32[]{:S(2)}, u32[]{:S(2)}) collective-permute-start(bf16[128,1,4096]{2,0,1:T(8,128)(2,1)} %get-tuple-element.27), channel_id=1, source_target_pairs={{8,0},{16,8},{24,16},{32,24},{40,32},{48,40},{56,48},{64,56},{72,6... | collective-permute-start | bytes 3145736 | tf_op jit(solution)/shard_map/ppermute | solution.py:15
  93.3 7.9 %copy-start = (bf16[1,128,16384]{1,0,2:T(2,128)(2,1)S(1)}, bf16[1,128,16384]{1,0,2:T(2,128)(2,1)}, u32[]{:S(2)}) copy-start(bf16[1,128,16384]{1,0,2:T(2,128)(2,1)} %copy.66) | copy-start | bytes 12582916
  101.2 42.6 %copy-start.6 = (u32[128]{0:T(128)S(1)}, u32[128]{0:T(128)}, u32[]{:S(2)}) copy-start(u32[128]{0:T(128)} %constant.69) | copy-start | bytes 1540
  131.5 28.6 %all-to-all-start = ((bf16[128,8,320]{2,1,0:T(8,128)(2,1)}), bf16[128,8,320]{2,1,0:T(8,128)(2,1)S(1)}, u32[]{:S(2)}, u32[]{:S(2)}) async-start(bf16[128,8,320]{2,1,0:T(8,128)(2,1)} %bitcast.24), calls=%async_computation | async-start | bytes 1572864 | tf_op jit(solution)/shard_map/all_to_all | solution.py:73
  143.8 165.9 %all-reduce.10.cloned.1.call-start = ((), (), s32[]{:S(2)}) async-start(), calls=%async_computation.3 | async-start | bytes 2621440
  165.6 226.1 %all-reduce.8.cloned.1.call-start = ((), (), s32[]{:S(2)}) async-start(), calls=%async_computation.2 | async-start | bytes 262144
Sparse Core Ops, SparseCore 0:
  12.2 88.5 all-gather.1
Sparse Core Ops, SparseCore 1:
  165.7 144.0 all-reduce.9
  313.1 78.6 all-reduce.7
where the time goes:
time: 403 us; the launch traced here: 401 us
  waiting for transfers between devices  229 us (57%)
  local copies, waits for them, and re-layouts  78.9 us (20%)
  other arithmetic  44.1 us (11%)
  starting transfers between devices  18.3 us (5%)
  between operations  16.5 us (4%)
  matrix products  14.4 us (4%)
    unnamed x5, waiting for transfers between devices  211 us
    unnamed x23, local copies, waits for them, and re-layouts  28 us
    another operation x1, other arithmetic, per_device(): rate = jnp.stack([sub_rate, bio_rate]).astype(jnp.bfloat16)  20.3 us
    another operation x2, local copies, waits for them, and re-layouts, per_device(): rate = jnp.stack([sub_rate, bio_rate]).astype(jnp.bfloat16)  16.5 us
    all_to_all x1, waiting for transfers between devices, per_device(): lax.all_to_all(send_buffer, ('grid', 'mode'), split_axis=0, concat_axis=0...  15.1 us
    another operation x4, local copies, waits for them, and re-layouts  12.7 us
    all_to_all x1, starting transfers between devices, per_device(): lax.all_to_all(send_buffer, ('grid', 'mode'), split_axis=0, concat_axis=0...  12.2 us
    dot_general x1, matrix products, per_device(): jnp.einsum('skrc,snrc->kn', lax.all_gather(basis, 'mode', axis=1, tiled=T...  12 us
  transfers between devices with their start and end apart: 6, of which 4 were waited for; matrix products, arithmetic and copies ran while one was open for 32% of the time, Pallas kernels for 0%

commit v1 on v0

v1 whole, which is shorter than its diff:
```python
import functools

import jax
import jax.numpy as jnp
from jax import lax
from jax.experimental import pallas as pl
from jax.experimental.pallas import tpu as pltpu
from jax.sharding import PartitionSpec as P

MESH = pl.DeviceIdType.MESH
F32 = jnp.float32
BF16 = jnp.bfloat16


def dot_nt(a, b):
    return lax.dot_general(a, b, (((1,), (1,)), ((), ())), preferred_element_type=F32)


def kernel(
    ng, nm, weight,
    state, basis, mask, cell_row, own_row,
    o_red, o_samp, o_gram, o_proj,
    raw_b, raw_s, st, rate, gat, hot, cellb, slots,
    acc_p, acc_b, picks, pbg, t1, t1r, w32, w16, w16r, hb, hr, mb, mr, fb, fr,
    lsem, ssem, rsem, hsem, psem, tsem, wsem, qsem, msem, fsem,
):
    g = lax.axis_index("grid")
    m = lax.axis_index("mode")
    ny = nm // 2
    c = lax.rem(m, 2)
    y = m // 2
    right = lax.rem(y + 1, ny) * 2 + c
    left = lax.rem(y + ny - 1, ny) * 2 + c
    opp = lax.rem(y + 2, ny) * 2 + c
    sib = y * 2 + (1 - c)
    flip = 1 - 2 * c
    modes = basis.shape[1]
    snaps = state.shape[1]
    nrow = state.shape[2]
    ncol = state.shape[3]
    samp = cell_row.shape[1]
    nchunk = 2 * nrow

    loads = []
    for s in range(2):
        loads.append(pltpu.make_async_copy(basis.at[s], raw_b.at[s], lsem.at[s]))
    for s in range(2):
        loads.append(pltpu.make_async_copy(state.at[s], raw_s.at[s], lsem.at[2 + s]))
    for load in loads:
        load.start()

    barrier = pltpu.get_barrier_semaphore()
    for d in range(1, nm):
        pl.semaphore_signal(barrier, inc=1, device_id=(g, lax.rem(m + d, nm)), device_id_type=MESH)
    for d in range(1, ng):
        pl.semaphore_signal(barrier, inc=1, device_id=(lax.rem(g + d, ng), m), device_id_type=MESH)
    pl.semaphore_wait(barrier, nm - 1 + ng - 1)

    sent = []

    def push(src, dst, send_sem, recv_sem, device):
        copy = pltpu.make_async_remote_copy(
            src_ref=src, dst_ref=dst, send_sem=send_sem, recv_sem=recv_sem,
            device_id=device, device_id_type=MESH,
        )
        copy.start()
        sent.append(copy)

    def await_recv(dst, send_sem, recv_sem):
        pltpu.make_async_remote_copy(
            src_ref=dst, dst_ref=dst, send_sem=send_sem, recv_sem=recv_sem,
            device_id=(g, sib), device_id_type=MESH,
        ).wait_recv()

    def ag_send(owner, j, kind, to):
        push(gat.at[j, owner], gat.at[j, owner], ssem.at[kind, j], rsem.at[owner, j], (g, to))

    def ag_recv(owner, j):
        await_recv(gat.at[j, owner], ssem.at[0, j], rsem.at[owner, j])

    def serve(j):
        ag_recv(left, j)
        if j % 2 == 0:
            ag_send(left, j, 3, right)
        ag_send(left, j, 4, sib)
        ag_recv(right, j)
        if j % 2 == 1:
            ag_send(right, j, 3, left)
        ag_send(right, j, 5, sib)

    for s in range(2):
        loads[s].wait()
        gat[pl.ds(s * nrow, nrow), m] = jnp.swapaxes(raw_b[s], 0, 1)
        for j in range(s * nrow, (s + 1) * nrow):
            ag_send(m, j, 0, right)
            ag_send(m, j, 1, left)
            ag_send(m, j, 2, sib)

    step = 16
    loads[2].wait()

    def split_s(i, carry):
        rows = pl.ds(pl.multiple_of(i * step, step), step)
        st[pl.ds(1, nrow), rows] = jnp.swapaxes(raw_s[0, rows], 0, 1)
        return carry

    lax.fori_loop(0, snaps // step, split_s, 0)
    up_dev = lax.rem(g + 1, ng)
    down_dev = lax.rem(g + ng - 1, ng)
    push(st.at[nrow], st.at[0], hsem.at[0], hsem.at[1], (up_dev, m))
    push(st.at[1], st.at[nrow + 1], hsem.at[2], hsem.at[3], (down_dev, m))
    loads[3].wait()

    def split_b(i, carry):
        rows = pl.ds(pl.multiple_of(i * step, step), step)
        high = pl.ds(pl.multiple_of(i * step + snaps, step), step)
        rate[:, high] = jnp.swapaxes(raw_s[1, rows], 0, 1)
        return carry

    lax.fori_loop(0, snaps // step, split_b, 0)

    lane = lax.broadcasted_iota(jnp.int32, (step, ncol), 1)

    def rates(r):
        film = jnp.broadcast_to(mask[pl.ds(r, 1), :].astype(F32), (step, ncol))
        up_on = jnp.where(jnp.logical_and(r == 0, g == 0), 0.0, 1.0).astype(F32)
        down_on = jnp.where(jnp.logical_and(r == nrow - 1, g == ng - 1), 0.0, 1.0).astype(F32)

        def body(i, carry):
            rows = pl.ds(pl.multiple_of(i * step, step), step)
            high = pl.ds(pl.multiple_of(i * step + snaps, step), step)
            sub = st[r + 1, rows].astype(F32)
            up = st[r, rows].astype(F32) * up_on
            down = st[r + 2, rows].astype(F32) * down_on
            bio = rate[r, high].astype(F32)
            before = jnp.where(lane == 0, 0.0, pltpu.roll(sub, 1, 1))
            after = jnp.where(lane == ncol - 1, 0.0, pltpu.roll(sub, ncol - 1, 1))
            lap = down + up + after + before - 4.0 * sub
            taken = bio * (sub / (0.5 + sub))
            rate[r, rows] = ((1.0 - 0.2 * film) * lap - 2.0 * taken).astype(BF16)
            rate[r, high] = (film * (taken - 0.1 * bio)).astype(BF16)
            return carry

        lax.fori_loop(0, snaps // step, body, 0)

    for r in range(1, nrow - 1):
        rates(r)
    serve(0)
    await_recv(st.at[0], hsem.at[0], hsem.at[1])
    await_recv(st.at[nrow + 1], hsem.at[2], hsem.at[3])
    rates(0)
    serve(1)
    rates(nrow - 1)
    serve(2)

    ii = lax.broadcasted_iota(jnp.int32, (samp, samp), 0)
    jj = lax.broadcasted_iota(jnp.int32, (samp, samp), 1)
    own = jnp.broadcast_to(own_row[...].astype(F32), (samp, samp))
    cel = jnp.broadcast_to(cell_row[...].astype(F32), (samp, samp))
    cell_col = jnp.sum(jnp.where(ii == jj, cel, 0.0), axis=1, keepdims=True)
    own_col = jnp.sum(jnp.where(ii == jj, own, 0.0), axis=1, keepdims=True)
    cellb[...] = jnp.broadcast_to(cell_col, cellb.shape)
    same = jnp.logical_and(own == own_col, ii < jj)
    rank = jnp.sum(jnp.where(same, 1.0, 0.0), axis=0, keepdims=True)
    own_f = own_row[...].astype(F32)
    own_hi = jnp.floor(own_f * (1.0 / nm))
    key = (own_f - own_hi * nm) * 128.0 + own_hi * 8.0 + rank
    for mm in range(nm):
        number = lax.broadcasted_iota(jnp.int32, (128, samp), 0).astype(F32) + float(mm * 128)
        slots[mm] = jnp.where(number == key, 1.0, 0.0).astype(BF16)

    lanes = lax.broadcasted_iota(jnp.int32, (samp, 128), 1).astype(F32)
    for r in range(nrow):
        def build(i, carry):
            base = (r * ncol + i * 128).astype(F32)
            cols = pl.ds(pl.multiple_of(i * 128, 128), 128)
            hot[:, cols] = jnp.where(cellb[...] == lanes + base, 1.0, 0.0).astype(BF16)
            return carry

        lax.fori_loop(0, ncol // 128, build, 0)
        part = dot_nt(rate[r], hot[...])
        acc_p[...] = part if r == 0 else acc_p[...] + part
        for s in range(2):
            part = dot_nt(gat[s * nrow + r, m], hot[...])
            acc_b[s] = part if r == 0 else acc_b[s] + part
        serve(3 + r)
    picks[...] = acc_p[...].astype(BF16)
    pbg[m] = acc_b[...].astype(BF16)
    for d in range(1, nm):
        to = lax.rem(m + d, nm)
        push(pbg.at[m], pbg.at[m], psem.at[0, d], psem.at[1, d], (g, to))
    for mm in range(nm):
        t1[mm] = dot_nt(slots[mm], picks[...]).astype(BF16)
    t1r[m] = t1[m]
    for d in range(1, nm):
        to = lax.rem(m + d, nm)
        push(t1.at[to], t1r.at[m], tsem.at[0, d], tsem.at[1, d], (g, to))
    serve(nchunk - 1)

    for d in range(1, nm):
        frm = lax.rem(m + nm - d, nm)
        await_recv(pbg.at[frm], psem.at[0, d], psem.at[1, d])

    hyper = jnp.zeros((nm * modes, snaps), F32)
    gram = jnp.zeros((nm * modes, modes), F32)
    for s in range(2):
        all_modes = pbg[:, s].reshape(nm * modes, samp)
        hyper = hyper + dot_nt(all_modes, picks[s * snaps : (s + 1) * snaps, :])
        gram = gram + dot_nt(all_modes, pbg[m, s])
        w32[:, 0:8, s * 256 : (s + 1) * 256] = dot_nt(slots[m], all_modes).reshape(ng, 8, nm * modes)
    hb[...] = jnp.zeros(hb.shape, F32)
    hb[:, :, 0:128] = (weight * hyper).reshape(ng, 16, snaps)
    hb[:, :, 128 : 128 + modes] = (weight * gram).reshape(ng, 16, modes)
    for d in range(1, ng):
        to = lax.rem(g + d, ng)
        push(hb.at[to], hr.at[g], qsem.at[0, d], qsem.at[1, d], (to, m))
    hr[g] = hb[g]

    for d in range(1, nm):
        frm = lax.rem(m + nm - d, nm)
        await_recv(t1r.at[frm], tsem.at[0, d], tsem.at[1, d])
    half = w32.shape[2]
    for mm in range(nm):
        for s in range(2):
            col = 2 * nm * modes + s * nm * snaps + mm * snaps
            block = t1r[mm, :, s * snaps : (s + 1) * snaps].astype(F32).reshape(ng, 8, snaps)
            if col < half:
                w32[:, 0:8, col : col + snaps] = block
            else:
                w32[:, 8:16, col - half : col - half + snaps] = block
    w16[...] = w32[...].astype(BF16)
    for d in range(1, ng):
        to = lax.rem(g + d, ng)
        push(w16.at[to], w16r.at[g], wsem.at[0, d], wsem.at[1, d], (to, m))
    w16r[g] = w16[g]

    for j in range(nchunk // 2):
        ag_recv(opp, j)
        ag_send(opp, j, 6, sib)

    for d in range(1, ng):
        frm = lax.rem(g + ng - d, ng)
        await_recv(hr.at[frm], qsem.at[0, d], qsem.at[1, d])
    total = jnp.sum(hr[...], axis=0)
    mb[...] = jnp.zeros(mb.shape, F32)
    for mm in range(nm):
        mb[mm, 0:2, :] = total[2 * mm : 2 * mm + 2, :]
    for d in range(1, nm):
        to = lax.rem(m + d, nm)
        push(mb.at[to], mr.at[m], msem.at[0, d], msem.at[1, d], (g, to))
    mr[m] = mb[m]

    fb[...] = jnp.zeros(fb.shape, F32)

    def project(j):
        s, r = j // nrow, j % nrow
        for owner in (sib, right + flip, left + flip, opp + flip):
            ag_recv(owner, j)
        block = gat[j].reshape(nm * modes, ncol)
        part = dot_nt(block, rate[r, s * snaps : (s + 1) * snaps, :])
        fb[...] += part.reshape(fb.shape)

    for j in range(nchunk // 2):
        project(j)
    for d in range(1, ng):
        frm = lax.rem(g + ng - d, ng)
        await_recv(w16r.at[frm], wsem.at[0, d], wsem.at[1, d])
    for h in range(2):
        part = w16r[...].astype(F32)[:, 8 * h : 8 * h + 8, :].reshape(ng * 8, half)
        o_samp[0, :, h * half : (h + 1) * half] = part.astype(BF16)
    for d in range(1, nm):
        frm = lax.rem(m + nm - d, nm)
        await_recv(mr.at[frm], msem.at[0, d], msem.at[1, d])
    for mm in range(nm):
        o_proj[:, mm * snaps : (mm + 1) * snaps] = mr[mm, 0:2, 0:snaps]
        o_gram[:, mm * modes : (mm + 1) * modes] = mr[mm, 0:2, 128 : 128 + modes]
    for j in range(nchunk // 2, nchunk):
        ag_recv(opp, j)
        ag_send(opp, j, 6, sib)
    for j in range(nchunk // 2, nchunk):
        project(j)

    for d in range(1, ng):
        to = lax.rem(g + d, ng)
        push(fb.at[to], fr.at[g], fsem.at[0, d], fsem.at[1, d], (to, m))
    fr[g] = fb[g]
    for d in range(1, ng):
        frm = lax.rem(g + ng - d, ng)
        await_recv(fr.at[frm], fsem.at[0, d], fsem.at[1, d])
    o_red[...] = jnp.sum(fr[...], axis=0)
    for copy in sent:
        copy.wait_send()


def per_device(ng, nm, state, film_mask, basis, sample_cells, owner):
    modes, snaps = basis.shape[1], state.shape[1]
    nrow, ncol = state.shape[2:]
    samp = sample_cells.shape[1]
    nchunk = 2 * nrow
    width = 2 * nm * (modes + snaps)
    dma = pltpu.SemaphoreType.DMA
    vmem = pl.BlockSpec(memory_space=pltpu.VMEM)
    hbm = pl.BlockSpec(memory_space=pl.ANY)
    return pl.pallas_call(
        functools.partial(kernel, ng, nm, nrow * ncol / samp),
        out_shape=(
            jax.ShapeDtypeStruct((nm * modes // ng, snaps), F32),
            jax.ShapeDtypeStruct((1, ng * 8, width), BF16),
            jax.ShapeDtypeStruct((2, nm * modes), F32),
            jax.ShapeDtypeStruct((2, nm * snaps), F32),
        ),
        in_specs=[hbm, hbm, vmem, vmem, vmem],
        out_specs=(vmem, vmem, vmem, vmem),
        scratch_shapes=[
            pltpu.VMEM((2, modes, nrow, ncol), BF16),
            pltpu.VMEM((2, snaps, nrow, ncol), BF16),
            pltpu.VMEM((nrow + 2, snaps, ncol), BF16),
            pltpu.VMEM((nrow, 2 * snaps, ncol), BF16),
            pltpu.VMEM((nchunk, nm, modes, ncol), BF16),
            pltpu.VMEM((samp, ncol), BF16),
            pltpu.VMEM((samp, 128), F32),
            pltpu.VMEM((nm, 128, samp), BF16),
            pltpu.VMEM((2 * snaps, samp), F32),
            pltpu.VMEM((2, modes, samp), F32),
            pltpu.VMEM((2 * snaps, samp), BF16),
            pltpu.VMEM((nm, 2, modes, samp), BF16),
            pltpu.VMEM((nm, 128, 2 * snaps), BF16),
            pltpu.VMEM((nm, 128, 2 * snaps), BF16),
            pltpu.VMEM((ng, 16, width // 2), F32),
            pltpu.VMEM((ng, 16, width // 2), BF16),
            pltpu.VMEM((ng, 16, width // 2), BF16),
            pltpu.VMEM((ng, 16, 256), F32),
            pltpu.VMEM((ng, 16, 256), F32),
            pltpu.VMEM((nm, 8, 256), F32),
            pltpu.VMEM((nm, 8, 256), F32),
            pltpu.VMEM((ng, nm * modes // ng, snaps), F32),
            pltpu.VMEM((ng, nm * modes // ng, snaps), F32),
            dma((4,)),
            dma((7, nchunk)),
            dma((nm, nchunk)),
            dma((4,)),
            dma((2, nm)),
            dma((2, nm)),
            dma((2, ng)),
            dma((2, ng)),
            dma((2, nm)),
            dma((2, ng)),
        ],
        compiler_params=pltpu.CompilerParams(
            collective_id=0, has_side_effects=True, vmem_limit_bytes=62 << 20
        ),
    )(state, basis, film_mask, sample_cells, owner.reshape(1, samp))


def solution(mesh):
    in_specs = (
        P(None, "mode", "grid", None),
        P("grid", None),
        P(None, "mode", "grid", None),
        P("grid", None),
        P("grid", None, None),
    )
    out_specs = (
        P("grid", "mode"),
        P(("grid", "mode"), None, None),
        P(("grid", "mode"), None),
        P(("grid", "mode"), None),
    )
    return jax.shard_map(
        functools.partial(per_device, mesh.shape["grid"], mesh.shape["mode"]),
        mesh=mesh, in_specs=in_specs, out_specs=out_specs, check_vma=False,
    )
```

time: 403 us -> 125 us (0.31)
  waiting for transfers between devices: 229 us -> 0 us
  Pallas kernels: 0 us -> 118 us
  local copies, waits for them, and re-layouts: 78.9 us -> 5.8 us
  other arithmetic: 44.1 us -> 0 us
  starting transfers between devices: 18.3 us -> 0 us
  between operations: 16.5 us -> 0.64 us
  matrix products: 14.4 us -> 0 us
    unnamed x5 -> x0, waiting for transfers between devices: 211 us -> none
    pallas_call x0 -> x1, Pallas kernels: none -> 118 us  [per_device(): pl.pallas_call(functools.partial(kernel, ng, nm, nrow * ncol / samp), out...]
    another operation x4 -> x0, other arithmetic: 32.2 us -> none  [the longest x1 20.3 us: per_device(): rate = jnp.stack([sub_rate, bio_rate]).astype(jnp.bfloat16)]
    another operation x8 -> x0, local copies, waits for them, and re-layouts: 29.9 us -> none  [the longest x2 16.5 us: per_device(): rate = jnp.stack([sub_rate, bio_rate]).astype(jnp.bfloat16)]
    unnamed x23 -> x4, local copies, waits for them, and re-layouts: 28 us -> 5.8 us
    all_to_all x1 -> x0, waiting for transfers between devices: 15.1 us -> none  [per_device(): lax.all_to_all(send_buffer, ('grid', 'mode'), split_axis=0, concat_axis=0...]
    dot_general x3 -> x0, matrix products: 14.4 us -> none  [the longest x1 12 us: per_device(): jnp.einsum('skrc,snrc->kn', lax.all_gather(basis, 'mode', axis=1, tiled=T...]
    all_to_all x1 -> x0, starting transfers between devices: 12.2 us -> none  [per_device(): lax.all_to_all(send_buffer, ('grid', 'mode'), split_axis=0, concat_axis=0...]
  transfers between devices with their start and end apart: 6 -> 0, of which waited for: 4 -> 0; matrix products, arithmetic and copies ran while one was open for 32% -> 0% of each run, Pallas kernels for 0% -> 0%
where the time goes in v1:
time: 125 us; the launch traced here: 124 us
  Pallas kernels  118 us (94%)
  local copies, waits for them, and re-layouts  5.8 us (5%)
    pallas_call x1, Pallas kernels, per_device(): pl.pallas_call(functools.partial(kernel, ng, nm, nrow * ncol / samp), out...  118 us
    unnamed x4, local copies, waits for them, and re-layouts  5.8 us

profile of v1, /device:TPU:1, one launch (start us, length us, event | category | flops | bytes accessed | tf_op | source)
XLA Modules:
  0.0 124.4 jit_solution(13508866192728836809)
XLA Ops:
  0.6 118.0 %shard_map.84 = (f32[16,128]{1,0:T(8,128)}, bf16[1,128,2560]{2,1,0:T(8,128)(2,1)}, f32[2,256]{1,0:T(2,128)}, f32[2,1024]{1,0:T(2,128)}) custom-call(bf16[2,128,4,4096]{3,2,1,0:T(4,128)(2,1)} %state.1, bf16[2,32,4,4096]{3,2,1,0:T(4,128)(2,1)} %basis.1, s32[4,4096]{1,0:T(4,128)} %mask.1, s32[1,512]{1,0:T(1,128)} %cell_row.1, s32[1,512]{1,0:T(1,128)} %bitcast.1), custom_call_target="tpu_custom_call" | custom-call | tf_op jit(solution)/shard_map/pallas_call | solution.py:304
  118.6 1.3 %copy.13 = f32[16,128]{1,0:T(8,128)} copy(f32[16,128]{1,0:T(8,128)} %get-tuple-element.8) | data formatting | bytes 16384
  119.9 2.0 %copy.14 = bf16[1,128,2560]{2,1,0:T(8,128)(2,1)} copy(bf16[1,128,2560]{2,1,0:T(8,128)(2,1)} %get-tuple-element.9) | data formatting | bytes 1310720
  121.9 1.2 copy.15
  123.1 1.3 %copy.16 = f32[2,1024]{1,0:T(2,128)} copy(f32[2,1024]{1,0:T(2,128)} %get-tuple-element.11) | data formatting | bytes 16384

commit v2 on v1

--- a/solution.py
+++ b/solution.py
@@ -20,9 +20,9 @@
     ng, nm, weight,
     state, basis, mask, cell_row, own_row,
     o_red, o_samp, o_gram, o_proj,
-    raw_b, raw_s, st, rate, gat, hot, cellb, slots,
-    acc_p, acc_b, picks, pbg, t1, t1r, w32, w16, w16r, hb, hr, mb, mr, fb, fr,
-    lsem, ssem, rsem, hsem, psem, tsem, wsem, qsem, msem, fsem,
+    raw_b, raw_s, st, rate, gat, hot, slots,
+    acc_p, picks, pbg, t1, t1r, relay, w32, w16, w16r, hb, hr, mb, mr, fb, fr,
+    lsem, ssem, rsem, hsem, tsem, wsem, qsem, msem, fsem,
 ):
     g = lax.axis_index("grid")
     m = lax.axis_index("mode")
@@ -46,8 +46,8 @@
         loads.append(pltpu.make_async_copy(basis.at[s], raw_b.at[s], lsem.at[s]))
     for s in range(2):
         loads.append(pltpu.make_async_copy(state.at[s], raw_s.at[s], lsem.at[2 + s]))
-    for load in loads:
-        load.start()
+    loads[0].start()
+    loads[1].start()
 
     barrier = pltpu.get_barrier_semaphore()
     for d in range(1, nm):
@@ -72,29 +72,59 @@
             device_id=(g, sib), device_id_type=MESH,
         ).wait_recv()
 
+    def slot(j, owner):
+        return gat.at[j, owner] if j < nchunk else pbg.at[j - nchunk, owner]
+
     def ag_send(owner, j, kind, to):
-        push(gat.at[j, owner], gat.at[j, owner], ssem.at[kind, j], rsem.at[owner, j], (g, to))
+        push(slot(j, owner), slot(j, owner), ssem.at[kind, j], rsem.at[owner, j], (g, to))
 
     def ag_recv(owner, j):
-        await_recv(gat.at[j, owner], ssem.at[0, j], rsem.at[owner, j])
-
-    def serve(j):
+        await_recv(slot(j, owner), ssem.at[0, j], rsem.at[owner, j])
+
+    def start(j):
+        ag_send(m, j, 0, right)
+        ag_send(m, j, 1, left)
+
+    def near(j):
         ag_recv(left, j)
+        ag_send(left, j, 4, sib)
+        ag_recv(right, j)
+        ag_send(right, j, 5, sib)
+
+    def onward(j):
         if j % 2 == 0:
             ag_send(left, j, 3, right)
-        ag_send(left, j, 4, sib)
-        ag_recv(right, j)
-        if j % 2 == 1:
+        else:
             ag_send(right, j, 3, left)
-        ag_send(right, j, 5, sib)
+
+    def far(j):
+        ag_recv(opp, j)
+        ag_send(opp, j, 6, sib)
+
+    def wait_sib(j):
+        for owner in (sib, right + flip, left + flip, opp + flip):
+            ag_recv(owner, j)
+
+    def project(j):
+        s, r = j // nrow, j % nrow
+        wait_sib(j)
+        block = gat[j].reshape(nm * modes, ncol)
+        part = dot_nt(block, rate[r, s * snaps : (s + 1) * snaps, :])
+        fb[...] += part.reshape(fb.shape)
 
     for s in range(2):
         loads[s].wait()
-        gat[pl.ds(s * nrow, nrow), m] = jnp.swapaxes(raw_b[s], 0, 1)
+        if s == 0:
+            loads[2].start()
+            loads[3].start()
+        mine = jnp.swapaxes(raw_b[s], 0, 1)
+        gat[pl.ds(s * nrow, nrow), m] = mine
         for j in range(s * nrow, (s + 1) * nrow):
-            ag_send(m, j, 0, right)
-            ag_send(m, j, 1, left)
-            ag_send(m, j, 2, sib)
+            if j < nchunk - 2:
+                start(j)
+        rate[:, 2 * snaps + s * modes : 2 * snaps + (s + 1) * modes] = mine
+    for j in range(nchunk):
+        ag_send(m, j, 2, sib)
 
     step = 16
     loads[2].wait()
@@ -143,23 +173,34 @@
 
         lax.fori_loop(0, snaps // step, body, 0)
 
-    for r in range(1, nrow - 1):
-        rates(r)
-    serve(0)
-    await_recv(st.at[0], hsem.at[0], hsem.at[1])
-    await_recv(st.at[nrow + 1], hsem.at[2], hsem.at[3])
-    rates(0)
-    serve(1)
-    rates(nrow - 1)
-    serve(2)
+    cells = cell_row[...].astype(F32)
+    part_rows = 512
+
+    def pick(r):
+        def build(i, carry):
+            base = (r * ncol + i * part_rows).astype(F32)
+            number = lax.broadcasted_iota(jnp.int32, (part_rows, samp), 0).astype(F32) + base
+            rows = pl.ds(pl.multiple_of(i * part_rows, part_rows), part_rows)
+            hot[rows] = jnp.where(number == cells, 1.0, 0.0).astype(BF16)
+            return carry
+
+        lax.fori_loop(0, ncol // part_rows, build, 0)
+        acc_p[...] += jnp.dot(rate[r], hot[...], preferred_element_type=F32)
+
+    acc_p[...] = jnp.zeros(acc_p.shape, F32)
+    fb[...] = jnp.zeros(fb.shape, F32)
+    rates(1)
+    near(0)
+    rates(2)
+    pick(1)
+    near(1)
+    pick(2)
+    near(2)
 
     ii = lax.broadcasted_iota(jnp.int32, (samp, samp), 0)
     jj = lax.broadcasted_iota(jnp.int32, (samp, samp), 1)
     own = jnp.broadcast_to(own_row[...].astype(F32), (samp, samp))
-    cel = jnp.broadcast_to(cell_row[...].astype(F32), (samp, samp))
-    cell_col = jnp.sum(jnp.where(ii == jj, cel, 0.0), axis=1, keepdims=True)
     own_col = jnp.sum(jnp.where(ii == jj, own, 0.0), axis=1, keepdims=True)
-    cellb[...] = jnp.broadcast_to(cell_col, cellb.shape)
     same = jnp.logical_and(own == own_col, ii < jj)
     rank = jnp.sum(jnp.where(same, 1.0, 0.0), axis=0, keepdims=True)
     own_f = own_row[...].astype(F32)
@@ -169,44 +210,69 @@
         number = lax.broadcasted_iota(jnp.int32, (128, samp), 0).astype(F32) + float(mm * 128)
         slots[mm] = jnp.where(number == key, 1.0, 0.0).astype(BF16)
 
-    lanes = lax.broadcasted_iota(jnp.int32, (samp, 128), 1).astype(F32)
-    for r in range(nrow):
-        def build(i, carry):
-            base = (r * ncol + i * 128).astype(F32)
-            cols = pl.ds(pl.multiple_of(i * 128, 128), 128)
-            hot[:, cols] = jnp.where(cellb[...] == lanes + base, 1.0, 0.0).astype(BF16)
-            return carry
-
-        lax.fori_loop(0, ncol // 128, build, 0)
-        part = dot_nt(rate[r], hot[...])
-        acc_p[...] = part if r == 0 else acc_p[...] + part
-        for s in range(2):
-            part = dot_nt(gat[s * nrow + r, m], hot[...])
-            acc_b[s] = part if r == 0 else acc_b[s] + part
-        serve(3 + r)
+    near(3)
+    onward(0)
+    onward(1)
+    await_recv(st.at[0], hsem.at[0], hsem.at[1])
+    await_recv(st.at[nrow + 1], hsem.at[2], hsem.at[3])
+    rates(0)
+    near(4)
+    pick(0)
+    rates(nrow - 1)
+    pick(nrow - 1)
     picks[...] = acc_p[...].astype(BF16)
-    pbg[m] = acc_b[...].astype(BF16)
-    for d in range(1, nm):
-        to = lax.rem(m + d, nm)
-        push(pbg.at[m], pbg.at[m], psem.at[0, d], psem.at[1, d], (g, to))
+    for s in range(2):
+        pbg[s, m] = picks[2 * snaps + s * modes : 2 * snaps + (s + 1) * modes, :]
     for mm in range(nm):
-        t1[mm] = dot_nt(slots[mm], picks[...]).astype(BF16)
+        t1[mm] = dot_nt(slots[mm], picks[0 : 2 * snaps, :]).astype(BF16)
+
+    def row_send(src, dst, n, origin, to):
+        push(src, dst, tsem.at[0, n], tsem.at[1, origin], (g, to))
+
+    def row_recv(dst, origin):
+        await_recv(dst, tsem.at[0, 0], tsem.at[1, origin])
+
+    for j in range(nchunk, nchunk + 2):
+        start(j)
+    row_send(t1.at[opp], relay.at[0], 0, nm, right)
+    row_send(t1.at[opp + flip], relay.at[1], 1, nm + 1, left)
+    row_send(t1.at[right], t1r.at[m], 2, m, right)
+    row_send(t1.at[left], t1r.at[m], 3, m, left)
+    row_send(t1.at[right + flip], t1r.at[m], 4, m, right + flip)
+    row_send(t1.at[left + flip], t1r.at[m], 5, m, left + flip)
+    start(nchunk - 2)
+    row_send(t1.at[sib], t1r.at[m], 6, m, sib)
+    for j in range(nchunk, nchunk + 2):
+        ag_send(m, j, 2, sib)
     t1r[m] = t1[m]
-    for d in range(1, nm):
-        to = lax.rem(m + d, nm)
-        push(t1.at[to], t1r.at[m], tsem.at[0, d], tsem.at[1, d], (g, to))
-    serve(nchunk - 1)
-
-    for d in range(1, nm):
-        frm = lax.rem(m + nm - d, nm)
-        await_recv(pbg.at[frm], psem.at[0, d], psem.at[1, d])
+    near(5)
+    far(0)
+    far(1)
+    project(0)
+    project(1)
+    for j in range(nchunk, nchunk + 2):
+        near(j)
+        onward(j)
+    row_recv(relay.at[0], nm)
+    row_send(relay.at[0], t1r.at[left], 7, left, right)
+    row_recv(relay.at[1], nm + 1)
+    row_send(relay.at[1], t1r.at[right], 8, right, left + flip)
+    start(nchunk - 1)
+    for j in range(2, 6):
+        onward(j)
+    near(6)
+    onward(6)
+    for j in range(nchunk, nchunk + 2):
+        far(j)
+    for j in range(nchunk, nchunk + 2):
+        wait_sib(j)
 
     hyper = jnp.zeros((nm * modes, snaps), F32)
     gram = jnp.zeros((nm * modes, modes), F32)
     for s in range(2):
-        all_modes = pbg[:, s].reshape(nm * modes, samp)
+        all_modes = pbg[s].reshape(nm * modes, samp)
         hyper = hyper + dot_nt(all_modes, picks[s * snaps : (s + 1) * snaps, :])
-        gram = gram + dot_nt(all_modes, pbg[m, s])
+        gram = gram + dot_nt(all_modes, pbg[s, m])
         w32[:, 0:8, s * 256 : (s + 1) * 256] = dot_nt(slots[m], all_modes).reshape(ng, 8, nm * modes)
     hb[...] = jnp.zeros(hb.shape, F32)
     hb[:, :, 0:128] = (weight * hyper).reshape(ng, 16, snaps)
@@ -216,9 +282,8 @@
         push(hb.at[to], hr.at[g], qsem.at[0, d], qsem.at[1, d], (to, m))
     hr[g] = hb[g]
 
-    for d in range(1, nm):
-        frm = lax.rem(m + nm - d, nm)
-        await_recv(t1r.at[frm], tsem.at[0, d], tsem.at[1, d])
+    for frm in (sib, right, right + flip, left, left + flip, opp, opp + flip):
+        row_recv(t1r.at[frm], frm)
     half = w32.shape[2]
     for mm in range(nm):
         for s in range(2):
@@ -234,10 +299,8 @@
         push(w16.at[to], w16r.at[g], wsem.at[0, d], wsem.at[1, d], (to, m))
     w16r[g] = w16[g]
 
-    for j in range(nchunk // 2):
-        ag_recv(opp, j)
-        ag_send(opp, j, 6, sib)
-
+    near(7)
+    onward(7)
     for d in range(1, ng):
         frm = lax.rem(g + ng - d, ng)
         await_recv(hr.at[frm], qsem.at[0, d], qsem.at[1, d])
@@ -249,19 +312,10 @@
         to = lax.rem(m + d, nm)
         push(mb.at[to], mr.at[m], msem.at[0, d], msem.at[1, d], (g, to))
     mr[m] = mb[m]
-
-    fb[...] = jnp.zeros(fb.shape, F32)
-
-    def project(j):
-        s, r = j // nrow, j % nrow
-        for owner in (sib, right + flip, left + flip, opp + flip):
-            ag_recv(owner, j)
-        block = gat[j].reshape(nm * modes, ncol)
-        part = dot_nt(block, rate[r, s * snaps : (s + 1) * snaps, :])
-        fb[...] += part.reshape(fb.shape)
-
-    for j in range(nchunk // 2):
-        project(j)
+    far(2)
+    far(3)
+    project(2)
+    project(3)
     for d in range(1, ng):
         frm = lax.rem(g + ng - d, ng)
         await_recv(w16r.at[frm], wsem.at[0, d], wsem.at[1, d])
@@ -274,11 +328,14 @@
     for mm in range(nm):
         o_proj[:, mm * snaps : (mm + 1) * snaps] = mr[mm, 0:2, 0:snaps]
         o_gram[:, mm * modes : (mm + 1) * modes] = mr[mm, 0:2, 128 : 128 + modes]
-    for j in range(nchunk // 2, nchunk):
-        ag_recv(opp, j)
-        ag_send(opp, j, 6, sib)
-    for j in range(nchunk // 2, nchunk):
-        project(j)
+    far(4)
+    far(5)
+    project(4)
+    project(5)
+    far(6)
+    far(7)
+    project(6)
+    project(7)
 
     for d in range(1, ng):
         to = lax.rem(g + d, ng)
@@ -290,6 +347,11 @@
     o_red[...] = jnp.sum(fr[...], axis=0)
     for copy in sent:
         copy.wait_send()
+
+
+def finish(*refs):
+    for source, target in zip(refs[:4], refs[4:]):
+        target[...] = source[...]
 
 
 def per_device(ng, nm, state, film_mask, basis, sample_cells, owner):
@@ -301,7 +363,7 @@
     dma = pltpu.SemaphoreType.DMA
     vmem = pl.BlockSpec(memory_space=pltpu.VMEM)
     hbm = pl.BlockSpec(memory_space=pl.ANY)
-    return pl.pallas_call(
+    outs = pl.pallas_call(
         functools.partial(kernel, ng, nm, nrow * ncol / samp),
         out_shape=(
             jax.ShapeDtypeStruct((nm * modes // ng, snaps), F32),
@@ -315,17 +377,16 @@
             pltpu.VMEM((2, modes, nrow, ncol), BF16),
             pltpu.VMEM((2, snaps, nrow, ncol), BF16),
             pltpu.VMEM((nrow + 2, snaps, ncol), BF16),
-            pltpu.VMEM((nrow, 2 * snaps, ncol), BF16),
+            pltpu.VMEM((nrow, 2 * (snaps + modes), ncol), BF16),
             pltpu.VMEM((nchunk, nm, modes, ncol), BF16),
-            pltpu.VMEM((samp, ncol), BF16),
-            pltpu.VMEM((samp, 128), F32),
+            pltpu.VMEM((ncol, samp), BF16),
             pltpu.VMEM((nm, 128, samp), BF16),
-            pltpu.VMEM((2 * snaps, samp), F32),
-            pltpu.VMEM((2, modes, samp), F32),
-            pltpu.VMEM((2 * snaps, samp), BF16),
-            pltpu.VMEM((nm, 2, modes, samp), BF16),
+            pltpu.VMEM((2 * (snaps + modes), samp), F32),
+            pltpu.VMEM((2 * (snaps + modes), samp), BF16),
+            pltpu.VMEM((2, nm, modes, samp), BF16),
             pltpu.VMEM((nm, 128, 2 * snaps), BF16),
             pltpu.VMEM((nm, 128, 2 * snaps), BF16),
+            pltpu.VMEM((2, 128, 2 * snaps), BF16),
             pltpu.VMEM((ng, 16, width // 2), F32),
             pltpu.VMEM((ng, 16, width // 2), BF16),
             pltpu.VMEM((ng, 16, width // 2), BF16),
@@ -336,11 +397,10 @@
             pltpu.VMEM((ng, nm * modes // ng, snaps), F32),
             pltpu.VMEM((ng, nm * modes // ng, snaps), F32),
             dma((4,)),
-            dma((7, nchunk)),
-            dma((nm, nchunk)),
+            dma((7, nchunk + 2)),
+            dma((nm, nchunk + 2)),
             dma((4,)),
-            dma((2, nm)),
-            dma((2, nm)),
+            dma((2, nm + 2)),
             dma((2, ng)),
             dma((2, ng)),
             dma((2, nm)),
@@ -350,6 +410,12 @@
             collective_id=0, has_side_effects=True, vmem_limit_bytes=62 << 20
         ),
     )(state, basis, film_mask, sample_cells, owner.reshape(1, samp))
+    return pl.pallas_call(
+        finish,
+        out_shape=tuple(jax.ShapeDtypeStruct(o.shape, o.dtype) for o in outs),
+        in_specs=[vmem] * 4,
+        out_specs=(vmem,) * 4,
+    )(*outs)
 
 
 def solution(mesh):

time: 125 us -> 105 us (0.84)
  Pallas kernels: 118 us -> 104 us
  local copies, waits for them, and re-layouts: 5.8 us -> 0 us
    pallas_call x1, Pallas kernels: 118 us -> 102 us  [per_device(): pl.pallas_call(functools.partial(kernel, ng, nm, nrow * ncol / samp), out...]
    unnamed x4 -> x0, local copies, waits for them, and re-layouts: 5.8 us -> none
    pallas_call x0 -> x1, Pallas kernels: none -> 1.98 us  [per_device(): pl.pallas_call(finish, out_shape=tuple((jax.ShapeDtypeStruct(o.shape, o.d...]
where the time goes in v2:
time: 105 us
  Pallas kernels  104 us (99%)
    pallas_call x1, Pallas kernels, per_device(): pl.pallas_call(functools.partial(kernel, ng, nm, nrow * ncol / samp), out...  102 us

profile of v2, /device:TPU:1, one launch (start us, length us, event | category | flops | bytes accessed | tf_op | source)
XLA Modules:
  0.0 105.0 jit_solution(15162631520555488439)
XLA Ops:
  0.6 102.3 %shard_map.84 = (f32[16,128]{1,0:T(8,128)}, bf16[1,128,2560]{2,1,0:T(8,128)(2,1)}, f32[2,256]{1,0:T(2,128)}, f32[2,1024]{1,0:T(2,128)}) custom-call(bf16[2,128,4,4096]{3,2,1,0:T(4,128)(2,1)} %state.1, bf16[2,32,4,4096]{3,2,1,0:T(4,128)(2,1)} %basis.1, s32[4,4096]{1,0:T(4,128)} %mask.1, s32[1,512]{1,0:T(1,128)} %cell_row.1, s32[1,512]{1,0:T(1,128)} %bitcast.1), custom_call_target="tpu_custom_call" | custom-call | tf_op jit(solution)/shard_map/pallas_call | solution.py:366
  103.0 2.0 %shard_map.85 = (f32[16,128]{1,0:T(8,128)}, bf16[1,128,2560]{2,1,0:T(8,128)(2,1)}, f32[2,256]{1,0:T(2,128)}, f32[2,1024]{1,0:T(2,128)}) custom-call(f32[16,128]{1,0:T(8,128)} %get-tuple-element.8.refs_0_, bf16[1,128,2560]{2,1,0:T(8,128)(2,1)} %get-tuple-element.9.refs_1_, f32[2,256]{1,0:T(2,128)} %get-tuple-element.10.refs_2_, ...), custom_call_target="tpu_custom_call" | custom-call | tf_op jit(solution)/shard_map/pallas_call | solution.py:413

commit v3 on v2

--- a/solution.py
+++ b/solution.py
@@ -21,8 +21,8 @@
     state, basis, mask, cell_row, own_row,
     o_red, o_samp, o_gram, o_proj,
     raw_b, raw_s, st, rate, gat, hot, slots,
-    acc_p, picks, pbg, t1, t1r, relay, w32, w16, w16r, hb, hr, mb, mr, fb, fr,
-    lsem, ssem, rsem, hsem, tsem, wsem, qsem, msem, fsem,
+    acc_p, picks, pbg, t0, t0r, t1, t1r, relay, w32, w16, w16r, hb, hr, mb, mr, acc_n, acc_f, fb, fr,
+    lsem, ssem, rsem, hsem, tsem, gsem, wsem, qsem, msem, fsem,
 ):
     g = lax.axis_index("grid")
     m = lax.axis_index("mode")
@@ -41,20 +41,22 @@
     samp = cell_row.shape[1]
     nchunk = 2 * nrow
 
-    loads = []
-    for s in range(2):
-        loads.append(pltpu.make_async_copy(basis.at[s], raw_b.at[s], lsem.at[s]))
-    for s in range(2):
-        loads.append(pltpu.make_async_copy(state.at[s], raw_s.at[s], lsem.at[2 + s]))
-    loads[0].start()
-    loads[1].start()
+    half_col = ncol // 2
+    loads = [
+        pltpu.make_async_copy(basis.at[0, :, :, 0:half_col], raw_b.at[0, :, :, 0:half_col], lsem.at[0]),
+        pltpu.make_async_copy(basis.at[0, :, :, half_col:ncol], raw_b.at[0, :, :, half_col:ncol], lsem.at[1]),
+        pltpu.make_async_copy(basis.at[1], raw_b.at[1], lsem.at[2]),
+        pltpu.make_async_copy(state.at[0], raw_s.at[0], lsem.at[3]),
+        pltpu.make_async_copy(state.at[1], raw_s.at[1], lsem.at[4]),
+    ]
+    for load in loads[:3]:
+        load.start()
 
     barrier = pltpu.get_barrier_semaphore()
     for d in range(1, nm):
         pl.semaphore_signal(barrier, inc=1, device_id=(g, lax.rem(m + d, nm)), device_id_type=MESH)
     for d in range(1, ng):
         pl.semaphore_signal(barrier, inc=1, device_id=(lax.rem(g + d, ng), m), device_id_type=MESH)
-    pl.semaphore_wait(barrier, nm - 1 + ng - 1)
 
     sent = []
 
@@ -72,62 +74,96 @@
             device_id=(g, sib), device_id_type=MESH,
         ).wait_recv()
 
-    def slot(j, owner):
-        return gat.at[j, owner] if j < nchunk else pbg.at[j - nchunk, owner]
-
-    def ag_send(owner, j, kind, to):
-        push(slot(j, owner), slot(j, owner), ssem.at[kind, j], rsem.at[owner, j], (g, to))
-
-    def ag_recv(owner, j):
-        await_recv(slot(j, owner), ssem.at[0, j], rsem.at[owner, j])
+    pieces = [(k, 2, col, half_col) for col in (0, half_col) for k in (0, 2)]
+    pieces += [(k, 1, 0, ncol) for k in (4, 5)]
+    pieces += [(k, 1, col, half_col) for col in (0, half_col) for k in (6, 7)]
+    npiece = len(pieces)
+    seen = (m, right, left, opp)
+
+    def slot(j, rel, owner):
+        if j < npiece:
+            k, count, col, size = pieces[j]
+            return gat.at[k : k + count, rel, c, :, col : col + size]
+        return pbg.at[j - npiece, owner]
+
+    def slot_sib(j, rel):
+        if j < npiece:
+            k, count, col, size = pieces[j]
+            return gat.at[k : k + count, rel, 1 - c, :, col : col + size]
+        return pbg.at[j - npiece, seen[rel] + flip]
+
+    def ag_send(j, rel, there, kind, to):
+        push(
+            slot(j, rel, seen[rel]), slot(j, there, seen[rel]),
+            ssem.at[kind, j], rsem.at[there, c, j], (g, to),
+        )
+
+    def ag_recv(j, rel):
+        await_recv(slot(j, rel, seen[rel]), ssem.at[0, j], rsem.at[rel, c, j])
 
     def start(j):
-        ag_send(m, j, 0, right)
-        ag_send(m, j, 1, left)
+        ag_send(j, 0, 2, 0, right)
+        ag_send(j, 0, 1, 1, left)
 
     def near(j):
-        ag_recv(left, j)
-        ag_send(left, j, 4, sib)
-        ag_recv(right, j)
-        ag_send(right, j, 5, sib)
+        ag_recv(j, 2)
+        ag_send(j, 2, 2, 4, sib)
+        ag_recv(j, 1)
+        ag_send(j, 1, 1, 5, sib)
 
     def onward(j):
         if j % 2 == 0:
-            ag_send(left, j, 3, right)
+            ag_send(j, 2, 3, 3, right)
         else:
-            ag_send(right, j, 3, left)
+            ag_send(j, 1, 3, 3, left)
 
     def far(j):
-        ag_recv(opp, j)
-        ag_send(opp, j, 6, sib)
-
-    def wait_sib(j):
-        for owner in (sib, right + flip, left + flip, opp + flip):
-            ag_recv(owner, j)
-
-    def project(j):
-        s, r = j // nrow, j % nrow
-        wait_sib(j)
-        block = gat[j].reshape(nm * modes, ncol)
-        part = dot_nt(block, rate[r, s * snaps : (s + 1) * snaps, :])
-        fb[...] += part.reshape(fb.shape)
-
-    for s in range(2):
-        loads[s].wait()
-        if s == 0:
-            loads[2].start()
-            loads[3].start()
-        mine = jnp.swapaxes(raw_b[s], 0, 1)
-        gat[pl.ds(s * nrow, nrow), m] = mine
-        for j in range(s * nrow, (s + 1) * nrow):
-            if j < nchunk - 2:
-                start(j)
-        rate[:, 2 * snaps + s * modes : 2 * snaps + (s + 1) * modes] = mine
-    for j in range(nchunk):
-        ag_send(m, j, 2, sib)
+        ag_recv(j, 3)
+        ag_send(j, 3, 3, 6, sib)
+
+    def wait_sib(j, rels):
+        for rel in rels:
+            await_recv(slot_sib(j, rel), ssem.at[0, j], rsem.at[rel, 1 - c, j])
+
+    def project(j, acc, low, high):
+        first, count, col, size = pieces[j]
+        wait_sib(j, range(low, high))
+        for k in range(first, first + count):
+            s, r = k // nrow, k % nrow
+            block = gat[k, low:high, :, :, col : col + size].reshape(acc.shape[0], size)
+            acc[...] += dot_nt(block, rate[r, s * snaps : (s + 1) * snaps, col : col + size])
+
+    def project_near(j):
+        project(j, acc_n, 0, 3)
+
+    def project_far(j):
+        project(j, acc_f, 3, 4)
+
+    def split_basis(s, col, size):
+        mine = jnp.swapaxes(raw_b[s, :, :, col : col + size], 0, 1)
+        gat[pl.ds(s * nrow, nrow), 0, c, :, col : col + size] = mine
+        rate[:, 2 * snaps + s * modes : 2 * snaps + (s + 1) * modes, col : col + size] = mine
+
+    loads[0].wait()
+    split_basis(0, 0, half_col)
+    pl.semaphore_wait(barrier, nm - 1 + ng - 1)
+    start(0)
+    start(1)
+    loads[1].wait()
+    split_basis(0, half_col, half_col)
+    start(2)
+    start(3)
+    loads[2].wait()
+    loads[3].start()
+    loads[4].start()
+    split_basis(1, 0, ncol)
+    start(4)
+    start(5)
+    for j in range(npiece):
+        ag_send(j, 0, 0, 2, sib)
 
     step = 16
-    loads[2].wait()
+    loads[3].wait()
 
     def split_s(i, carry):
         rows = pl.ds(pl.multiple_of(i * step, step), step)
@@ -139,7 +175,7 @@
     down_dev = lax.rem(g + ng - 1, ng)
     push(st.at[nrow], st.at[0], hsem.at[0], hsem.at[1], (up_dev, m))
     push(st.at[1], st.at[nrow + 1], hsem.at[2], hsem.at[3], (down_dev, m))
-    loads[3].wait()
+    loads[4].wait()
 
     def split_b(i, carry):
         rows = pl.ds(pl.multiple_of(i * step, step), step)
@@ -188,7 +224,8 @@
         acc_p[...] += jnp.dot(rate[r], hot[...], preferred_element_type=F32)
 
     acc_p[...] = jnp.zeros(acc_p.shape, F32)
-    fb[...] = jnp.zeros(fb.shape, F32)
+    acc_n[...] = jnp.zeros(acc_n.shape, F32)
+    acc_f[...] = jnp.zeros(acc_f.shape, F32)
     rates(1)
     near(0)
     rates(2)
@@ -205,10 +242,14 @@
     rank = jnp.sum(jnp.where(same, 1.0, 0.0), axis=0, keepdims=True)
     own_f = own_row[...].astype(F32)
     own_hi = jnp.floor(own_f * (1.0 / nm))
-    key = (own_f - own_hi * nm) * 128.0 + own_hi * 8.0 + rank
-    for mm in range(nm):
-        number = lax.broadcasted_iota(jnp.int32, (128, samp), 0).astype(F32) + float(mm * 128)
-        slots[mm] = jnp.where(number == key, 1.0, 0.0).astype(BF16)
+    own_lo = own_f - own_hi * nm
+    key = own_f * 8.0 + rank
+    for gg in range(ng):
+        number = lax.broadcasted_iota(jnp.int32, (8 * nm, samp), 0).astype(F32) + float(gg * 8 * nm)
+        slots[gg] = jnp.where(number == key, 1.0, 0.0).astype(BF16)
+    key = jnp.where(own_lo == m.astype(F32), own_hi * 8.0 + rank, -1.0)
+    number = lax.broadcasted_iota(jnp.int32, (8 * ng, samp), 0).astype(F32)
+    mine = jnp.where(number == key, 1.0, 0.0).astype(BF16)
 
     near(3)
     onward(0)
@@ -223,8 +264,19 @@
     picks[...] = acc_p[...].astype(BF16)
     for s in range(2):
         pbg[s, m] = picks[2 * snaps + s * modes : 2 * snaps + (s + 1) * modes, :]
-    for mm in range(nm):
-        t1[mm] = dot_nt(slots[mm], picks[0 : 2 * snaps, :]).astype(BF16)
+    picked = (npiece, npiece + 1)
+    for j in picked:
+        start(j)
+    start(6)
+    start(7)
+    for j in picked:
+        ag_send(j, 0, 0, 2, sib)
+    rows = dot_nt(slots[...].reshape(8 * nm * ng, samp), picks[0 : 2 * snaps, :])
+    t0[...] = rows.astype(BF16).reshape(t0.shape)
+    for d in range(1, ng):
+        to = lax.rem(g + d, ng)
+        push(t0.at[to], t0r.at[g], gsem.at[0, d], gsem.at[1, d], (to, m))
+    t0r[g] = t0[g]
 
     def row_send(src, dst, n, origin, to):
         push(src, dst, tsem.at[0, n], tsem.at[1, origin], (g, to))
@@ -232,40 +284,28 @@
     def row_recv(dst, origin):
         await_recv(dst, tsem.at[0, 0], tsem.at[1, origin])
 
-    for j in range(nchunk, nchunk + 2):
-        start(j)
-    row_send(t1.at[opp], relay.at[0], 0, nm, right)
-    row_send(t1.at[opp + flip], relay.at[1], 1, nm + 1, left)
-    row_send(t1.at[right], t1r.at[m], 2, m, right)
-    row_send(t1.at[left], t1r.at[m], 3, m, left)
-    row_send(t1.at[right + flip], t1r.at[m], 4, m, right + flip)
-    row_send(t1.at[left + flip], t1r.at[m], 5, m, left + flip)
-    start(nchunk - 2)
-    row_send(t1.at[sib], t1r.at[m], 6, m, sib)
-    for j in range(nchunk, nchunk + 2):
-        ag_send(m, j, 2, sib)
-    t1r[m] = t1[m]
     near(5)
+    for j in range(6):
+        project_near(j)
     far(0)
     far(1)
-    project(0)
-    project(1)
-    for j in range(nchunk, nchunk + 2):
+    for j in picked:
         near(j)
         onward(j)
-    row_recv(relay.at[0], nm)
-    row_send(relay.at[0], t1r.at[left], 7, left, right)
-    row_recv(relay.at[1], nm + 1)
-    row_send(relay.at[1], t1r.at[right], 8, right, left + flip)
-    start(nchunk - 1)
+    start(8)
+    start(9)
     for j in range(2, 6):
         onward(j)
+    project_far(0)
+    project_far(1)
     near(6)
     onward(6)
-    for j in range(nchunk, nchunk + 2):
+    near(7)
+    onward(7)
+    for j in picked:
         far(j)
-    for j in range(nchunk, nchunk + 2):
-        wait_sib(j)
+    for j in picked:
+        wait_sib(j, range(4))
 
     hyper = jnp.zeros((nm * modes, snaps), F32)
     gram = jnp.zeros((nm * modes, modes), F32)
@@ -273,7 +313,7 @@
         all_modes = pbg[s].reshape(nm * modes, samp)
         hyper = hyper + dot_nt(all_modes, picks[s * snaps : (s + 1) * snaps, :])
         gram = gram + dot_nt(all_modes, pbg[s, m])
-        w32[:, 0:8, s * 256 : (s + 1) * 256] = dot_nt(slots[m], all_modes).reshape(ng, 8, nm * modes)
+        w32[:, 8 * s : 8 * s + 8, :] = dot_nt(mine, all_modes).reshape(ng, 8, nm * modes)
     hb[...] = jnp.zeros(hb.shape, F32)
     hb[:, :, 0:128] = (weight * hyper).reshape(ng, 16, snaps)
     hb[:, :, 128 : 128 + modes] = (weight * gram).reshape(ng, 16, modes)
@@ -282,25 +322,22 @@
         push(hb.at[to], hr.at[g], qsem.at[0, d], qsem.at[1, d], (to, m))
     hr[g] = hb[g]
 
-    for frm in (sib, right, right + flip, left, left + flip, opp, opp + flip):
-        row_recv(t1r.at[frm], frm)
-    half = w32.shape[2]
-    for mm in range(nm):
-        for s in range(2):
-            col = 2 * nm * modes + s * nm * snaps + mm * snaps
-            block = t1r[mm, :, s * snaps : (s + 1) * snaps].astype(F32).reshape(ng, 8, snaps)
-            if col < half:
-                w32[:, 0:8, col : col + snaps] = block
-            else:
-                w32[:, 8:16, col - half : col - half + snaps] = block
     w16[...] = w32[...].astype(BF16)
     for d in range(1, ng):
         to = lax.rem(g + d, ng)
         push(w16.at[to], w16r.at[g], wsem.at[0, d], wsem.at[1, d], (to, m))
     w16r[g] = w16[g]
 
-    near(7)
-    onward(7)
+    for d in range(1, ng):
+        frm = lax.rem(g + ng - d, ng)
+        await_recv(t0r.at[frm], gsem.at[0, d], gsem.at[1, d])
+    for mm in range(nm):
+        t1[mm] = t0r[...].astype(F32)[:, 8 * mm : 8 * mm + 8, :].reshape(ng * 8, 2 * snaps).astype(BF16)
+    near(8)
+    onward(8)
+    near(9)
+    onward(9)
+    settled = len(sent) - 6
     for d in range(1, ng):
         frm = lax.rem(g + ng - d, ng)
         await_recv(hr.at[frm], qsem.at[0, d], qsem.at[1, d])
@@ -312,35 +349,80 @@
         to = lax.rem(m + d, nm)
         push(mb.at[to], mr.at[m], msem.at[0, d], msem.at[1, d], (g, to))
     mr[m] = mb[m]
+    row_send(t1.at[opp], relay.at[0], 0, nm, right)
+    row_send(t1.at[opp + flip], relay.at[1], 1, nm + 1, left)
+    row_send(t1.at[right], t1r.at[m], 2, m, right)
+    row_send(t1.at[left], t1r.at[m], 3, m, left)
+    row_send(t1.at[right + flip], t1r.at[m], 4, m, right + flip)
+    row_send(t1.at[left + flip], t1r.at[m], 5, m, left + flip)
+    row_send(t1.at[sib], t1r.at[m], 6, m, sib)
+    t1r[m] = t1[m]
+    for j in range(6, 10):
+        project_near(j)
+
+    per_chip = ng // ny
+    opp_chip = lax.rem(y + 2, ny)
+    for rel in range(3):
+        fb[pl.ds(per_chip * (seen[rel] // 2), per_chip)] = acc_n[
+            rel * 2 * modes : (rel + 1) * 2 * modes
+        ].reshape(per_chip, fb.shape[1], snaps)
+
+    def sums(late):
+        for d in range(1, ng):
+            to = lax.rem(g + d, ng)
+            copy = pltpu.make_async_remote_copy(
+                src_ref=fb.at[to], dst_ref=fr.at[g], send_sem=fsem.at[0, d], recv_sem=fsem.at[1, d],
+                device_id=(to, m), device_id_type=MESH,
+            )
+            pl.when((to // per_chip == opp_chip) == late)(copy.start)
+            if late:
+                sent.append(copy)
+
+    sums(False)
     far(2)
     far(3)
-    project(2)
-    project(3)
+    project_far(2)
+    project_far(3)
     for d in range(1, ng):
         frm = lax.rem(g + ng - d, ng)
         await_recv(w16r.at[frm], wsem.at[0, d], wsem.at[1, d])
-    for h in range(2):
-        part = w16r[...].astype(F32)[:, 8 * h : 8 * h + 8, :].reshape(ng * 8, half)
-        o_samp[0, :, h * half : (h + 1) * half] = part.astype(BF16)
+    for s in range(2):
+        part = w16r[...].astype(F32)[:, 8 * s : 8 * s + 8, :].reshape(ng * 8, nm * modes)
+        o_samp[0, :, s * nm * modes : (s + 1) * nm * modes] = part.astype(BF16)
+    far(4)
+    far(5)
+    project_far(4)
+    project_far(5)
+    for copy in sent[:settled]:
+        copy.wait_send()
+    del sent[:settled]
+    far(6)
+    far(7)
+    project_far(6)
+    project_far(7)
+    far(8)
+    far(9)
+    row_recv(relay.at[0], nm)
+    row_send(relay.at[0], t1r.at[left], 7, left, right)
+    row_recv(relay.at[1], nm + 1)
+    row_send(relay.at[1], t1r.at[right], 8, right, left + flip)
+    project_far(8)
+    project_far(9)
+    fb[pl.ds(per_chip * opp_chip, per_chip)] = acc_f[...].reshape(per_chip, fb.shape[1], snaps)
+    sums(True)
+    fr[g] = fb[g]
+    for frm in (sib, right, right + flip, left, left + flip, opp, opp + flip):
+        row_recv(t1r.at[frm], frm)
+    for mm in range(nm):
+        for s in range(2):
+            col = 2 * nm * modes + s * nm * snaps + mm * snaps
+            o_samp[0, :, col : col + snaps] = t1r[mm, :, s * snaps : (s + 1) * snaps]
     for d in range(1, nm):
         frm = lax.rem(m + nm - d, nm)
         await_recv(mr.at[frm], msem.at[0, d], msem.at[1, d])
     for mm in range(nm):
         o_proj[:, mm * snaps : (mm + 1) * snaps] = mr[mm, 0:2, 0:snaps]
         o_gram[:, mm * modes : (mm + 1) * modes] = mr[mm, 0:2, 128 : 128 + modes]
-    far(4)
-    far(5)
-    project(4)
-    project(5)
-    far(6)
-    far(7)
-    project(6)
-    project(7)
-
-    for d in range(1, ng):
-        to = lax.rem(g + d, ng)
-        push(fb.at[to], fr.at[g], fsem.at[0, d], fsem.at[1, d], (to, m))
-    fr[g] = fb[g]
     for d in range(1, ng):
         frm = lax.rem(g + ng - d, ng)
         await_recv(fr.at[frm], fsem.at[0, d], fsem.at[1, d])
@@ -378,36 +460,41 @@
             pltpu.VMEM((2, snaps, nrow, ncol), BF16),
             pltpu.VMEM((nrow + 2, snaps, ncol), BF16),
             pltpu.VMEM((nrow, 2 * (snaps + modes), ncol), BF16),
-            pltpu.VMEM((nchunk, nm, modes, ncol), BF16),
+            pltpu.VMEM((nchunk, nm // 2, 2, modes, ncol), BF16),
             pltpu.VMEM((ncol, samp), BF16),
-            pltpu.VMEM((nm, 128, samp), BF16),
+            pltpu.VMEM((ng, 8 * nm, samp), BF16),
             pltpu.VMEM((2 * (snaps + modes), samp), F32),
             pltpu.VMEM((2 * (snaps + modes), samp), BF16),
             pltpu.VMEM((2, nm, modes, samp), BF16),
-            pltpu.VMEM((nm, 128, 2 * snaps), BF16),
-            pltpu.VMEM((nm, 128, 2 * snaps), BF16),
+            pltpu.VMEM((ng, 8 * nm, 2 * snaps), BF16),
+            pltpu.VMEM((ng, 8 * nm, 2 * snaps), BF16),
+            pltpu.VMEM((nm, 8 * ng, 2 * snaps), BF16),
+            pltpu.VMEM((nm, 8 * ng, 2 * snaps), BF16),
             pltpu.VMEM((2, 128, 2 * snaps), BF16),
-            pltpu.VMEM((ng, 16, width // 2), F32),
-            pltpu.VMEM((ng, 16, width // 2), BF16),
-            pltpu.VMEM((ng, 16, width // 2), BF16),
+            pltpu.VMEM((ng, 16, nm * modes), F32),
+            pltpu.VMEM((ng, 16, nm * modes), BF16),
+            pltpu.VMEM((ng, 16, nm * modes), BF16),
             pltpu.VMEM((ng, 16, 256), F32),
             pltpu.VMEM((ng, 16, 256), F32),
             pltpu.VMEM((nm, 8, 256), F32),
             pltpu.VMEM((nm, 8, 256), F32),
+            pltpu.VMEM((6 * modes, snaps), F32),
+            pltpu.VMEM((2 * modes, snaps), F32),
             pltpu.VMEM((ng, nm * modes // ng, snaps), F32),
             pltpu.VMEM((ng, nm * modes // ng, snaps), F32),
-            dma((4,)),
-            dma((7, nchunk + 2)),
-            dma((nm, nchunk + 2)),
+            dma((5,)),
+            dma((7, nchunk + 4)),
+            dma((4, 2, nchunk + 4)),
             dma((4,)),
             dma((2, nm + 2)),
+            dma((2, ng)),
             dma((2, ng)),
             dma((2, ng)),
             dma((2, nm)),
             dma((2, ng)),
         ],
         compiler_params=pltpu.CompilerParams(
-            collective_id=0, has_side_effects=True, vmem_limit_bytes=62 << 20
+            collective_id=0, has_side_effects=True, vmem_limit_bytes=56 << 20
         ),
     )(state, basis, film_mask, sample_cells, owner.reshape(1, samp))
     return pl.pallas_call(

time: 105 us -> 94.3 us (0.90)
  Pallas kernels: 104 us -> 93.4 us
    pallas_call x1, Pallas kernels: 102 us -> 91.4 us  [per_device(): pl.pallas_call(functools.partial(kernel, ng, nm, nrow * ncol / samp), out...]
where the time goes in v3:
time: 94.3 us; the launch traced here: 94 us
  Pallas kernels  93.4 us (99%)
    pallas_call x1, Pallas kernels, per_device(): pl.pallas_call(functools.partial(kernel, ng, nm, nrow * ncol / samp), out...  91.4 us
    pallas_call x1, Pallas kernels, per_device(): pl.pallas_call(finish, out_shape=tuple((jax.ShapeDtypeStruct(o.shape, o.d...  1.98 us

profile of v3, /device:TPU:1, one launch (start us, length us, event | category | flops | bytes accessed | tf_op | source)
XLA Modules:
  0.0 94.0 jit_solution(9078976116730135892)
XLA Ops:
  0.6 91.4 %shard_map.84 = (f32[16,128]{1,0:T(8,128)}, bf16[1,128,2560]{2,1,0:T(8,128)(2,1)}, f32[2,256]{1,0:T(2,128)}, f32[2,1024]{1,0:T(2,128)}) custom-call(bf16[2,128,4,4096]{3,2,1,0:T(4,128)(2,1)} %state.1, bf16[2,32,4,4096]{3,2,1,0:T(4,128)(2,1)} %basis.1, s32[4,4096]{1,0:T(4,128)} %mask.1, s32[1,512]{1,0:T(1,128)} %cell_row.1, s32[1,512]{1,0:T(1,128)} %bitcast.1), custom_call_target="tpu_custom_call" | custom-call | tf_op jit(solution)/shard_map/pallas_call | solution.py:448
  92.0 2.0 %shard_map.85 = (f32[16,128]{1,0:T(8,128)}, bf16[1,128,2560]{2,1,0:T(8,128)(2,1)}, f32[2,256]{1,0:T(2,128)}, f32[2,1024]{1,0:T(2,128)}) custom-call(f32[16,128]{1,0:T(8,128)} %get-tuple-element.8.refs_0_, bf16[1,128,2560]{2,1,0:T(8,128)(2,1)} %get-tuple-element.9.refs_1_, f32[2,256]{1,0:T(2,128)} %get-tuple-element.10.refs_2_, ...), custom_call_target="tpu_custom_call" | custom-call | tf_op jit(solution)/shard_map/pallas_call | solution.py:500

commit v4 on v3

--- a/solution.py
+++ b/solution.py
@@ -18,11 +18,11 @@
 
 def kernel(
     ng, nm, weight,
-    state, basis, mask, cell_row, own_row,
+    state, basis, mask_in, cells_in, owner_in,
     o_red, o_samp, o_gram, o_proj,
-    raw_b, raw_s, st, rate, gat, hot, slots,
+    mask, cell_row, own_row, raw_b, raw_g, raw_s, st, rate, other, gat, hot, slots,
     acc_p, picks, pbg, t0, t0r, t1, t1r, relay, w32, w16, w16r, hb, hr, mb, mr, acc_n, acc_f, fb, fr,
-    lsem, ssem, rsem, hsem, tsem, gsem, wsem, qsem, msem, fsem,
+    lsem, ssem, rsem, hsem, tsem, gsem, wsem, qsem, msem, fsem, xsem,
 ):
     g = lax.axis_index("grid")
     m = lax.axis_index("mode")
@@ -38,7 +38,7 @@
     snaps = state.shape[1]
     nrow = state.shape[2]
     ncol = state.shape[3]
-    samp = cell_row.shape[1]
+    samp = cells_in.shape[1]
     nchunk = 2 * nrow
 
     half_col = ncol // 2
@@ -49,8 +49,11 @@
         pltpu.make_async_copy(state.at[0], raw_s.at[0], lsem.at[3]),
         pltpu.make_async_copy(state.at[1], raw_s.at[1], lsem.at[4]),
     ]
-    for load in loads[:3]:
-        load.start()
+    small = [
+        pltpu.make_async_copy(mask_in, mask, lsem.at[5]),
+        pltpu.make_async_copy(cells_in, cell_row, lsem.at[6]),
+        pltpu.make_async_copy(owner_in, own_row, lsem.at[7]),
+    ]
 
     barrier = pltpu.get_barrier_semaphore()
     for d in range(1, nm):
@@ -58,6 +61,8 @@
     for d in range(1, ng):
         pl.semaphore_signal(barrier, inc=1, device_id=(lax.rem(g + d, ng), m), device_id_type=MESH)
 
+    for load in loads[:3] + small:
+        load.start()
     sent = []
 
     def push(src, dst, send_sem, recv_sem, device):
@@ -74,27 +79,27 @@
             device_id=(g, sib), device_id_type=MESH,
         ).wait_recv()
 
-    pieces = [(k, 2, col, half_col) for col in (0, half_col) for k in (0, 2)]
+    pieces = [(0, 4, 0, half_col // 2), (0, 4, half_col // 2, half_col // 2)]
+    pieces += [(k, 2, half_col, half_col) for k in (0, 2)]
     pieces += [(k, 1, 0, ncol) for k in (4, 5)]
     pieces += [(k, 1, col, half_col) for col in (0, half_col) for k in (6, 7)]
     npiece = len(pieces)
     seen = (m, right, left, opp)
 
     def slot(j, rel, owner):
+        if j < 2:
+            return raw_g.at[rel, j]
         if j < npiece:
             k, count, col, size = pieces[j]
-            return gat.at[k : k + count, rel, c, :, col : col + size]
+            return gat.at[k : k + count, rel, :, col : col + size]
         return pbg.at[j - npiece, owner]
 
-    def slot_sib(j, rel):
-        if j < npiece:
-            k, count, col, size = pieces[j]
-            return gat.at[k : k + count, rel, 1 - c, :, col : col + size]
-        return pbg.at[j - npiece, seen[rel] + flip]
-
     def ag_send(j, rel, there, kind, to):
+        source = slot(j, rel, seen[rel])
+        if j < 2 and rel == 0:
+            source = basis.at[0, :, :, pieces[j][2] : pieces[j][2] + pieces[j][3]]
         push(
-            slot(j, rel, seen[rel]), slot(j, there, seen[rel]),
+            source, slot(j, there, seen[rel]),
             ssem.at[kind, j], rsem.at[there, c, j], (g, to),
         )
 
@@ -105,11 +110,17 @@
         ag_send(j, 0, 2, 0, right)
         ag_send(j, 0, 1, 1, left)
 
+    def unpack(j, rel):
+        if j < 2:
+            first, count, col, size = pieces[j]
+            gat[first : first + count, rel, :, col : col + size] = jnp.swapaxes(raw_g[rel, j], 0, 1)
+
     def near(j):
-        ag_recv(j, 2)
-        ag_send(j, 2, 2, 4, sib)
-        ag_recv(j, 1)
-        ag_send(j, 1, 1, 5, sib)
+        for rel, kind in ((2, 4), (1, 5)):
+            ag_recv(j, rel)
+            if j >= npiece:
+                ag_send(j, rel, rel, kind, sib)
+            unpack(j, rel)
 
     def onward(j):
         if j % 2 == 0:
@@ -119,19 +130,27 @@
 
     def far(j):
         ag_recv(j, 3)
-        ag_send(j, 3, 3, 6, sib)
-
-    def wait_sib(j, rels):
-        for rel in rels:
-            await_recv(slot_sib(j, rel), ssem.at[0, j], rsem.at[rel, 1 - c, j])
+        if j >= npiece:
+            ag_send(j, 3, 3, 6, sib)
+        unpack(j, 3)
+
+    def wait_sib(j):
+        for rel in range(4):
+            await_recv(pbg.at[j - npiece, seen[rel] + flip], ssem.at[0, j], rsem.at[rel, 1 - c, j])
 
     def project(j, acc, low, high):
         first, count, col, size = pieces[j]
-        wait_sib(j, range(low, high))
         for k in range(first, first + count):
             s, r = k // nrow, k % nrow
-            block = gat[k, low:high, :, :, col : col + size].reshape(acc.shape[0], size)
-            acc[...] += dot_nt(block, rate[r, s * snaps : (s + 1) * snaps, col : col + size])
+            block = gat[k, low:high, :, col : col + size].reshape(acc.shape[0], size)
+            both = jnp.concatenate(
+                [
+                    rate[r, s * snaps : (s + 1) * snaps, col : col + size],
+                    other[r, s * snaps : (s + 1) * snaps, col : col + size],
+                ],
+                axis=0,
+            )
+            acc[...] += dot_nt(block, both)
 
     def project_near(j):
         project(j, acc_n, 0, 3)
@@ -141,14 +160,14 @@
 
     def split_basis(s, col, size):
         mine = jnp.swapaxes(raw_b[s, :, :, col : col + size], 0, 1)
-        gat[pl.ds(s * nrow, nrow), 0, c, :, col : col + size] = mine
+        gat[pl.ds(s * nrow, nrow), 0, :, col : col + size] = mine
         rate[:, 2 * snaps + s * modes : 2 * snaps + (s + 1) * modes, col : col + size] = mine
 
-    loads[0].wait()
-    split_basis(0, 0, half_col)
     pl.semaphore_wait(barrier, nm - 1 + ng - 1)
     start(0)
     start(1)
+    loads[0].wait()
+    split_basis(0, 0, half_col)
     loads[1].wait()
     split_basis(0, half_col, half_col)
     start(2)
@@ -159,8 +178,6 @@
     split_basis(1, 0, ncol)
     start(4)
     start(5)
-    for j in range(npiece):
-        ag_send(j, 0, 0, 2, sib)
 
     step = 16
     loads[3].wait()
@@ -185,6 +202,8 @@
 
     lax.fori_loop(0, snaps // step, split_b, 0)
 
+    for load in small:
+        load.wait()
     lane = lax.broadcasted_iota(jnp.int32, (step, ncol), 1)
 
     def rates(r):
@@ -208,6 +227,7 @@
             return carry
 
         lax.fori_loop(0, snaps // step, body, 0)
+        push(rate.at[r, 0 : 2 * snaps], other.at[r], xsem.at[0, r], xsem.at[1, r], (g, sib))
 
     cells = cell_row[...].astype(F32)
     part_rows = 512
@@ -252,8 +272,8 @@
     mine = jnp.where(number == key, 1.0, 0.0).astype(BF16)
 
     near(3)
-    onward(0)
-    onward(1)
+    for j in range(4):
+        onward(j)
     await_recv(st.at[0], hsem.at[0], hsem.at[1])
     await_recv(st.at[nrow + 1], hsem.at[2], hsem.at[3])
     rates(0)
@@ -285,6 +305,8 @@
         await_recv(dst, tsem.at[0, 0], tsem.at[1, origin])
 
     near(5)
+    for r in range(nrow):
+        await_recv(other.at[r], xsem.at[0, r], xsem.at[1, r])
     for j in range(6):
         project_near(j)
     far(0)
@@ -294,7 +316,7 @@
         onward(j)
     start(8)
     start(9)
-    for j in range(2, 6):
+    for j in range(4, 6):
         onward(j)
     project_far(0)
     project_far(1)
@@ -305,7 +327,7 @@
     for j in picked:
         far(j)
     for j in picked:
-        wait_sib(j, range(4))
+        wait_sib(j)
 
     hyper = jnp.zeros((nm * modes, snaps), F32)
     gram = jnp.zeros((nm * modes, modes), F32)
@@ -338,6 +360,52 @@
     near(9)
     onward(9)
     settled = len(sent) - 6
+    row_send(t1.at[opp], relay.at[0], 0, nm, right)
+    row_send(t1.at[opp + flip], relay.at[1], 1, nm + 1, left)
+    row_send(t1.at[right], t1r.at[m], 2, m, right)
+    row_send(t1.at[left], t1r.at[m], 3, m, left)
+    row_send(t1.at[right + flip], t1r.at[m], 4, m, right + flip)
+    row_send(t1.at[left + flip], t1r.at[m], 5, m, left + flip)
+    row_send(t1.at[sib], t1r.at[m], 6, m, sib)
+    t1r[m] = t1[m]
+    for j in range(6, 10):
+        project_near(j)
+
+    def sums(acc, rels):
+        for n, rel in enumerate(rels):
+            for h in range(2):
+                to = seen[rel] // 2 * (ng // ny) + 2 * c + h
+                for t in range(2):
+                    low = modes * n + fb.shape[3] * h
+                    fb[t, rel, h] = acc[low : low + fb.shape[3], t * snaps : (t + 1) * snaps]
+                    copy = pltpu.make_async_remote_copy(
+                        src_ref=fb.at[t, rel, h], dst_ref=fr.at[g],
+                        send_sem=fsem.at[0, t * 8 + rel * 2 + h], recv_sem=fsem.at[1, g],
+                        device_id=(to, sib if t else m), device_id_type=MESH,
+                    )
+                    if t:
+                        copy.start()
+                        sent.append(copy)
+                    else:
+                        pl.when(to != g)(copy.start)
+                        last.append((to, copy))
+
+                        @pl.when(to == g)
+                        def _():
+                            fr[g] = fb[t, rel, h]
+
+    last = []
+    sums(acc_n, range(3))
+    far(2)
+    far(3)
+    project_far(2)
+    project_far(3)
+    for d in range(1, ng):
+        frm = lax.rem(g + ng - d, ng)
+        await_recv(w16r.at[frm], wsem.at[0, d], wsem.at[1, d])
+    for s in range(2):
+        part = w16r[...].astype(F32)[:, 8 * s : 8 * s + 8, :].reshape(ng * 8, nm * modes)
+        o_samp[0, :, s * nm * modes : (s + 1) * nm * modes] = part.astype(BF16)
     for d in range(1, ng):
         frm = lax.rem(g + ng - d, ng)
         await_recv(hr.at[frm], qsem.at[0, d], qsem.at[1, d])
@@ -349,46 +417,6 @@
         to = lax.rem(m + d, nm)
         push(mb.at[to], mr.at[m], msem.at[0, d], msem.at[1, d], (g, to))
     mr[m] = mb[m]
-    row_send(t1.at[opp], relay.at[0], 0, nm, right)
-    row_send(t1.at[opp + flip], relay.at[1], 1, nm + 1, left)
-    row_send(t1.at[right], t1r.at[m], 2, m, right)
-    row_send(t1.at[left], t1r.at[m], 3, m, left)
-    row_send(t1.at[right + flip], t1r.at[m], 4, m, right + flip)
-    row_send(t1.at[left + flip], t1r.at[m], 5, m, left + flip)
-    row_send(t1.at[sib], t1r.at[m], 6, m, sib)
-    t1r[m] = t1[m]
-    for j in range(6, 10):
-        project_near(j)
-
-    per_chip = ng // ny
-    opp_chip = lax.rem(y + 2, ny)
-    for rel in range(3):
-        fb[pl.ds(per_chip * (seen[rel] // 2), per_chip)] = acc_n[
-            rel * 2 * modes : (rel + 1) * 2 * modes
-        ].reshape(per_chip, fb.shape[1], snaps)
-
-    def sums(late):
-        for d in range(1, ng):
-            to = lax.rem(g + d, ng)
-            copy = pltpu.make_async_remote_copy(
-                src_ref=fb.at[to], dst_ref=fr.at[g], send_sem=fsem.at[0, d], recv_sem=fsem.at[1, d],
-                device_id=(to, m), device_id_type=MESH,
-            )
-            pl.when((to // per_chip == opp_chip) == late)(copy.start)
-            if late:
-                sent.append(copy)
-
-    sums(False)
-    far(2)
-    far(3)
-    project_far(2)
-    project_far(3)
-    for d in range(1, ng):
-        frm = lax.rem(g + ng - d, ng)
-        await_recv(w16r.at[frm], wsem.at[0, d], wsem.at[1, d])
-    for s in range(2):
-        part = w16r[...].astype(F32)[:, 8 * s : 8 * s + 8, :].reshape(ng * 8, nm * modes)
-        o_samp[0, :, s * nm * modes : (s + 1) * nm * modes] = part.astype(BF16)
     far(4)
     far(5)
     project_far(4)
@@ -408,9 +436,7 @@
     row_send(relay.at[1], t1r.at[right], 8, right, left + flip)
     project_far(8)
     project_far(9)
-    fb[pl.ds(per_chip * opp_chip, per_chip)] = acc_f[...].reshape(per_chip, fb.shape[1], snaps)
-    sums(True)
-    fr[g] = fb[g]
+    sums(acc_f, range(3, 4))
     for frm in (sib, right, right + flip, left, left + flip, opp, opp + flip):
         row_recv(t1r.at[frm], frm)
     for mm in range(nm):
@@ -423,12 +449,18 @@
     for mm in range(nm):
         o_proj[:, mm * snaps : (mm + 1) * snaps] = mr[mm, 0:2, 0:snaps]
         o_gram[:, mm * modes : (mm + 1) * modes] = mr[mm, 0:2, 128 : 128 + modes]
-    for d in range(1, ng):
-        frm = lax.rem(g + ng - d, ng)
-        await_recv(fr.at[frm], fsem.at[0, d], fsem.at[1, d])
+    mine_core = lax.rem(g // 2, 2) == c
+    for frm in range(ng):
+
+        @pl.when(jnp.logical_or(frm != g, jnp.logical_not(mine_core)))
+        def _():
+            await_recv(fr.at[frm], fsem.at[0, frm], fsem.at[1, frm])
+
     o_red[...] = jnp.sum(fr[...], axis=0)
     for copy in sent:
         copy.wait_send()
+    for to, copy in last:
+        pl.when(to != g)(copy.wait_send)
 
 
 def finish(*refs):
@@ -448,19 +480,24 @@
     outs = pl.pallas_call(
         functools.partial(kernel, ng, nm, nrow * ncol / samp),
         out_shape=(
-            jax.ShapeDtypeStruct((nm * modes // ng, snaps), F32),
-            jax.ShapeDtypeStruct((1, ng * 8, width), BF16),
-            jax.ShapeDtypeStruct((2, nm * modes), F32),
-            jax.ShapeDtypeStruct((2, nm * snaps), F32),
+            pltpu.VMEM((nm * modes // ng, snaps), F32),
+            pltpu.VMEM((1, ng * 8, width), BF16),
+            pltpu.VMEM((2, nm * modes), F32),
+            pltpu.VMEM((2, nm * snaps), F32),
         ),
-        in_specs=[hbm, hbm, vmem, vmem, vmem],
+        in_specs=[hbm] * 5,
         out_specs=(vmem, vmem, vmem, vmem),
         scratch_shapes=[
+            pltpu.VMEM((nrow, ncol), jnp.int32),
+            pltpu.VMEM((1, samp), jnp.int32),
+            pltpu.VMEM((1, samp), jnp.int32),
             pltpu.VMEM((2, modes, nrow, ncol), BF16),
+            pltpu.VMEM((nm // 2, 2, modes, nrow, ncol // 4), BF16),
             pltpu.VMEM((2, snaps, nrow, ncol), BF16),
             pltpu.VMEM((nrow + 2, snaps, ncol), BF16),
             pltpu.VMEM((nrow, 2 * (snaps + modes), ncol), BF16),
-            pltpu.VMEM((nchunk, nm // 2, 2, modes, ncol), BF16),
+            pltpu.VMEM((nrow, 2 * snaps, ncol), BF16),
+            pltpu.VMEM((nchunk, nm // 2, modes, ncol), BF16),
             pltpu.VMEM((ncol, samp), BF16),
             pltpu.VMEM((ng, 8 * nm, samp), BF16),
             pltpu.VMEM((2 * (snaps + modes), samp), F32),
@@ -478,11 +515,11 @@
             pltpu.VMEM((ng, 16, 256), F32),
             pltpu.VMEM((nm, 8, 256), F32),
             pltpu.VMEM((nm, 8, 256), F32),
-            pltpu.VMEM((6 * modes, snaps), F32),
-            pltpu.VMEM((2 * modes, snaps), F32),
+            pltpu.VMEM((3 * modes, 2 * snaps), F32),
+            pltpu.VMEM((modes, 2 * snaps), F32),
+            pltpu.VMEM((2, nm // 2, 2, nm * modes // ng, snaps), F32),
             pltpu.VMEM((ng, nm * modes // ng, snaps), F32),
-            pltpu.VMEM((ng, nm * modes // ng, snaps), F32),
-            dma((5,)),
+            dma((8,)),
             dma((7, nchunk + 4)),
             dma((4, 2, nchunk + 4)),
             dma((4,)),
@@ -492,9 +529,10 @@
             dma((2, ng)),
             dma((2, nm)),
             dma((2, ng)),
+            dma((2, nrow)),
         ],
         compiler_params=pltpu.CompilerParams(
-            collective_id=0, has_side_effects=True, vmem_limit_bytes=56 << 20
+            collective_id=0, has_side_effects=True, vmem_limit_bytes=59 << 20
         ),
     )(state, basis, film_mask, sample_cells, owner.reshape(1, samp))
     return pl.pallas_call(
@@ -502,7 +540,7 @@
         out_shape=tuple(jax.ShapeDtypeStruct(o.shape, o.dtype) for o in outs),
         in_specs=[vmem] * 4,
         out_specs=(vmem,) * 4,
-    )(*outs)
+    )(*[pltpu.with_memory_space_constraint(o, pltpu.VMEM) for o in outs])
 
 
 def solution(mesh):

time: 94.3 us -> 91.9 us (0.975)
  Pallas kernels: 93.4 us -> 91 us
    pallas_call x1, Pallas kernels: 91.4 us -> 90.1 us  [per_device(): pl.pallas_call(functools.partial(kernel, ng, nm, nrow * ncol / samp), out...]
    pallas_call x1, Pallas kernels: 1.98 us -> 0.88 us  [per_device(): pl.pallas_call(finish, out_shape=tuple((jax.ShapeDtypeStruct(o.shape, o.d...]
where the time goes in v4:
time: 91.9 us; the launch traced here: 91.6 us
  Pallas kernels  91 us (99%)
    pallas_call x1, Pallas kernels, per_device(): pl.pallas_call(functools.partial(kernel, ng, nm, nrow * ncol / samp), out...  90.1 us

profile of v4, /device:TPU:1, one launch (start us, length us, event | category | flops | bytes accessed | tf_op | source)
XLA Modules:
  0.0 91.6 jit_solution(6872246499148326333)
XLA Ops:
  0.6 90.1 %shard_map.84 = (f32[16,128]{1,0:T(8,128)S(1)}, bf16[1,128,2560]{2,1,0:T(8,128)(2,1)S(1)}, f32[2,256]{1,0:T(2,128)S(1)}, f32[2,1024]{1,0:T(2,128)S(1)}) custom-call(bf16[2,128,4,4096]{3,2,1,0:T(4,128)(2,1)} %state.1, bf16[2,32,4,4096]{3,2,1,0:T(4,128)(2,1)} %basis.1, s32[4,4096]{1,0:T(4,128)} %mask_in.1, s32[1,512]{1,0:T(1,128)} %cells_in.1, s32[1,512]{1,0:T(1,128)} %bitcast.1), custom_call_target="tpu_custom_call" | custom-call | tf_op jit(solution)/shard_map/pallas_call | solution.py:480
  90.8 0.9 shard_map.85

commit v5 on v4

--- a/solution.py
+++ b/solution.py
@@ -22,7 +22,7 @@
     o_red, o_samp, o_gram, o_proj,
     mask, cell_row, own_row, raw_b, raw_g, raw_s, st, rate, other, gat, hot, slots,
     acc_p, picks, pbg, t0, t0r, t1, t1r, relay, w32, w16, w16r, hb, hr, mb, mr, acc_n, acc_f, fb, fr,
-    lsem, ssem, rsem, hsem, tsem, gsem, wsem, qsem, msem, fsem, xsem,
+    lsem, ssem, rsem, hsem, tsem, gsem, wsem, qsem, msem, fsem, xsem, known,
 ):
     g = lax.axis_index("grid")
     m = lax.axis_index("mode")
@@ -55,11 +55,22 @@
         pltpu.make_async_copy(owner_in, own_row, lsem.at[7]),
     ]
 
+    up_dev = lax.rem(g + 1, ng)
+    down_dev = lax.rem(g + ng - 1, ng)
+    around = [(g, right), (g, left), (g, sib), (up_dev, m), (down_dev, m)]
     barrier = pltpu.get_barrier_semaphore()
-    for d in range(1, nm):
-        pl.semaphore_signal(barrier, inc=1, device_id=(g, lax.rem(m + d, nm)), device_id_type=MESH)
-    for d in range(1, ng):
-        pl.semaphore_signal(barrier, inc=1, device_id=(lax.rem(g + d, ng), m), device_id_type=MESH)
+    for dev in around:
+        pl.semaphore_signal(barrier, inc=1, device_id=dev, device_id_type=MESH)
+    rounds = [around]
+    rounds.append([(lax.rem(g + 2, ng), m), (lax.rem(g + ng - 2, ng), m), (g, sib)])
+    rounds.append([(lax.rem(g + 4, ng), m), (lax.rem(g + ng - 4, ng), m)])
+
+    def announce(n):
+        for dev in rounds[n]:
+            pl.semaphore_signal(known.at[n], inc=1, device_id=dev, device_id_type=MESH)
+
+    def heard(n):
+        pl.semaphore_wait(known.at[n], len(rounds[n]))
 
     for load in loads[:3] + small:
         load.start()
@@ -163,9 +174,10 @@
         gat[pl.ds(s * nrow, nrow), 0, :, col : col + size] = mine
         rate[:, 2 * snaps + s * modes : 2 * snaps + (s + 1) * modes, col : col + size] = mine
 
-    pl.semaphore_wait(barrier, nm - 1 + ng - 1)
+    pl.semaphore_wait(barrier, len(around))
     start(0)
     start(1)
+    announce(0)
     loads[0].wait()
     split_basis(0, 0, half_col)
     loads[1].wait()
@@ -188,8 +200,8 @@
         return carry
 
     lax.fori_loop(0, snaps // step, split_s, 0)
-    up_dev = lax.rem(g + 1, ng)
-    down_dev = lax.rem(g + ng - 1, ng)
+    heard(0)
+    announce(1)
     push(st.at[nrow], st.at[0], hsem.at[0], hsem.at[1], (up_dev, m))
     push(st.at[1], st.at[nrow + 1], hsem.at[2], hsem.at[3], (down_dev, m))
     loads[4].wait()
@@ -247,8 +259,11 @@
     acc_n[...] = jnp.zeros(acc_n.shape, F32)
     acc_f[...] = jnp.zeros(acc_f.shape, F32)
     rates(1)
+    heard(1)
+    announce(2)
     near(0)
     rates(2)
+    heard(2)
     pick(1)
     near(1)
     pick(2)
@@ -437,30 +452,38 @@
     project_far(8)
     project_far(9)
     sums(acc_f, range(3, 4))
-    for frm in (sib, right, right + flip, left, left + flip, opp, opp + flip):
+    def place(frm):
+        for s in range(2):
+            col = pl.multiple_of(2 * nm * modes + s * nm * snaps + frm * snaps, 128)
+            o_samp[0, :, pl.ds(col, snaps)] = t1r[frm, :, s * snaps : (s + 1) * snaps]
+
+    place(m)
+    row_recv(t1r.at[sib], sib)
+    place(sib)
+    for copy in sent:
+        copy.wait_send()
+    for to, copy in last:
+        pl.when(to != g)(copy.wait_send)
+    for frm in (right, right + flip, left, left + flip):
         row_recv(t1r.at[frm], frm)
-    for mm in range(nm):
-        for s in range(2):
-            col = 2 * nm * modes + s * nm * snaps + mm * snaps
-            o_samp[0, :, col : col + snaps] = t1r[mm, :, s * snaps : (s + 1) * snaps]
+        place(frm)
+    mine_core = lax.rem(g // 2, 2) == c
+    for frm in range(ng):
+
+        @pl.when(jnp.logical_or(frm != g, jnp.logical_not(mine_core)))
+        def _():
+            await_recv(fr.at[frm], fsem.at[0, frm], fsem.at[1, frm])
+
+    o_red[...] = jnp.sum(fr[...], axis=0)
+    for frm in (opp, opp + flip):
+        row_recv(t1r.at[frm], frm)
+        place(frm)
     for d in range(1, nm):
         frm = lax.rem(m + nm - d, nm)
         await_recv(mr.at[frm], msem.at[0, d], msem.at[1, d])
     for mm in range(nm):
         o_proj[:, mm * snaps : (mm + 1) * snaps] = mr[mm, 0:2, 0:snaps]
         o_gram[:, mm * modes : (mm + 1) * modes] = mr[mm, 0:2, 128 : 128 + modes]
-    mine_core = lax.rem(g // 2, 2) == c
-    for frm in range(ng):
-
-        @pl.when(jnp.logical_or(frm != g, jnp.logical_not(mine_core)))
-        def _():
-            await_recv(fr.at[frm], fsem.at[0, frm], fsem.at[1, frm])
-
-    o_red[...] = jnp.sum(fr[...], axis=0)
-    for copy in sent:
-        copy.wait_send()
-    for to, copy in last:
-        pl.when(to != g)(copy.wait_send)
 
 
 def finish(*refs):
@@ -530,6 +553,7 @@
             dma((2, nm)),
             dma((2, ng)),
             dma((2, nrow)),
+            pltpu.SemaphoreType.REGULAR((3,)),
         ],
         compiler_params=pltpu.CompilerParams(
             collective_id=0, has_side_effects=True, vmem_limit_bytes=59 << 20

time: 91.9 us -> 91.3 us (level)
  no operation moved by 1% of the time
where the time goes in v5:
time: 91.3 us; the launch traced here: 91.2 us
  Pallas kernels  90.6 us (99%)
    pallas_call x1, Pallas kernels, per_device(): pl.pallas_call(functools.partial(kernel, ng, nm, nrow * ncol / samp), out...  89.7 us

profile of v5, /device:TPU:1, one launch (start us, length us, event | category | flops | bytes accessed | tf_op | source)
XLA Modules:
  0.0 91.2 jit_solution(885806161871857685)
XLA Ops:
  0.6 89.7 %shard_map.84 = (f32[16,128]{1,0:T(8,128)S(1)}, bf16[1,128,2560]{2,1,0:T(8,128)(2,1)S(1)}, f32[2,256]{1,0:T(2,128)S(1)}, f32[2,1024]{1,0:T(2,128)S(1)}) custom-call(bf16[2,128,4,4096]{3,2,1,0:T(4,128)(2,1)} %state.1, bf16[2,32,4,4096]{3,2,1,0:T(4,128)(2,1)} %basis.1, s32[4,4096]{1,0:T(4,128)} %mask_in.1, s32[1,512]{1,0:T(1,128)} %cells_in.1, s32[1,512]{1,0:T(1,128)} %bitcast.1), custom_call_target="tpu_custom_call" | custom-call | tf_op jit(solution)/shard_map/pallas_call | solution.py:503
  90.3 0.9 shard_map.85
